TPU v7x, 32 devices: a whole 2x2x4 slice. The times are simulated.
32 devices in a mesh: seq: 4 (over x, core), head: 8 (over z, y).
Axes of the slice: x: 2, y: 2, z: 4, core: 2. Of those that a mesh axis runs over, the one named last changes fastest.
Arguments:
- query_heads: bfloat16 [512, 16, 128], P(('seq', 'head')), may hold values from -6 to 6
- key_heads: bfloat16 [512, 16, 128], P(('seq', 'head')), may hold values from -6 to 6
- value_heads: bfloat16 [512, 32, 128], P(('seq', 'head')), may hold values from -6 to 6
- gate_log: bfloat16 [512, 32], P(('seq', 'head')), may hold values from -1 to 0
- beta_rate: bfloat16 [512, 32], P(('seq', 'head')), may hold values from 0.0099487305 to 0.099609375
Outputs:
- head_output: bfloat16 [512, 4096], P(('seq', 'head'))
- block_states: float32 [4, 32, 128, 128], P('seq', 'head')
All inputs are finite; a program needn't handle non-finite values.
Results may differ from a plain program's by a relative error of at most 0.001.
Values may be sent and summed in bfloat16 or wider, within the bound.
A program may use at most 64 MiB of HBM per device.

v0:
```python
import jax
import jax.numpy as jnp
from jax import lax
from jax.sharding import PartitionSpec as P

STRETCH = 64


HIGHEST = lax.Precision.HIGHEST


def shifted(block, axis, distance):
    devices = range(lax.axis_size(axis))
    route = [(i - distance, i) for i in devices if i - distance in devices]
    return lax.ppermute(block, axis, route)


def normalize(tensor):
    tensor = tensor.astype(jnp.float32)
    return tensor / jnp.sqrt(jnp.sum(tensor * tensor, axis=-1, keepdims=True) + 1e-06)


def stretch_parts(queries, keys_in, values, gate_vals, beta_vals):
    span_len = gate_vals.shape[-1]
    cumulative = jnp.cumsum(gate_vals, axis=-1)
    row_ids = lax.broadcasted_iota(jnp.int32, (span_len, span_len), 0)
    columns = lax.broadcasted_iota(jnp.int32, (span_len, span_len), 1)
    strict = row_ids > columns
    inclusive = row_ids >= columns
    differ = cumulative[..., :, None] - cumulative[..., None, :]
    key_key = jnp.einsum("...rd,...sd->...rs", keys_in, keys_in, precision=HIGHEST)
    query_key = jnp.einsum("...rd,...sd->...rs", queries, keys_in, precision=HIGHEST)
    lower_triangle = jnp.where(
        strict, beta_vals[..., :, None] * jnp.exp(jnp.where(strict, differ, 0.0)) * key_key, 0.0
    )
    scores = jnp.where(inclusive, jnp.exp(jnp.where(inclusive, differ, 0.0)) * query_key, 0.0)
    identity = jnp.eye(span_len, dtype=jnp.float32)
    right_side = jnp.concatenate(
        [(beta_vals * jnp.exp(cumulative))[..., None] * keys_in, beta_vals[..., None] * values],
        axis=-1,
    )
    solved = jax.scipy.linalg.solve_triangular(
        identity + lower_triangle, right_side, lower=True, unit_diagonal=True
    )
    key_width = keys_in.shape[-1]
    last_cum = cumulative[..., -1:]
    query_dec = jnp.exp(cumulative)[..., None] * queries
    key_dec = jnp.exp(last_cum - cumulative)[..., None] * keys_in
    return (
        solved[..., :key_width],
        solved[..., key_width:],
        scores,
        query_dec,
        key_dec,
        jnp.exp(last_cum[..., 0]),
    )


def product(left_mat, right_mat):
    return jnp.einsum("...ij,...jk->...ik", left_mat, right_mat, precision=HIGHEST)


def compose(earlier, later):
    return (product(later[0], earlier[0]), product(later[0], earlier[1]) + later[1])


def slab_local(queries, keys_in, values, gate_vals, beta_vals):
    heads, length = gate_vals.shape
    blocks = length // STRETCH

    def split_rows(tensor):
        return tensor.reshape((heads, blocks, STRETCH) + tensor.shape[2:])

    write_keys, write_vals, scores, query_dec, key_dec, stretch_decay = stretch_parts(
        split_rows(queries),
        split_rows(keys_in),
        split_rows(values),
        split_rows(gate_vals),
        split_rows(beta_vals),
    )
    key_width = keys_in.shape[-1]
    identity = jnp.eye(key_width, dtype=jnp.float32)
    transit = stretch_decay[..., None, None] * identity - jnp.einsum(
        "hncd,hnce->hnde", key_dec, write_keys, precision=HIGHEST
    )
    inject = jnp.einsum("hncd,hnce->hnde", key_dec, write_vals, precision=HIGHEST)
    project = query_dec - jnp.einsum("hnrs,hnsd->hnrd", scores, write_keys, precision=HIGHEST)
    direct = jnp.einsum("hnrs,hnse->hnre", scores, write_vals, precision=HIGHEST)
    maps_all, states_all = lax.associative_scan(compose, (transit, inject), axis=1)
    reach_rest = product(project[:, 1:], maps_all[:, :-1])
    reach = jnp.concatenate([project[:, :1], reach_rest], axis=1).reshape(heads, length, key_width)
    out_rest = product(project[:, 1:], states_all[:, :-1]) + direct[:, 1:]
    local_out = jnp.concatenate([direct[:, :1], out_rest], axis=1).reshape(heads, length, -1)
    return (local_out, reach, maps_all[:, -1], states_all[:, -1])


def per_device(query_heads, key_heads, value_heads, gate_log, beta_rate):
    key_count = query_heads.shape[1]
    grouping = value_heads.shape[1] // key_count
    got_query, got_key, got_value, got_gate, got_beta = (
        lax.all_to_all(
            jnp.repeat(query_heads, grouping, axis=1),
            "head",
            split_axis=1,
            concat_axis=0,
            tiled=True,
        ),
        lax.all_to_all(
            jnp.repeat(key_heads, grouping, axis=1), "head", split_axis=1, concat_axis=0, tiled=True
        ),
        lax.all_to_all(value_heads, "head", split_axis=1, concat_axis=0, tiled=True),
        lax.all_to_all(gate_log, "head", split_axis=1, concat_axis=0, tiled=True),
        lax.all_to_all(beta_rate, "head", split_axis=1, concat_axis=0, tiled=True),
    )
    queries = jnp.swapaxes(normalize(got_query), 0, 1)
    keys_in = jnp.swapaxes(normalize(got_key), 0, 1)
    values = jnp.swapaxes(got_value.astype(jnp.float32), 0, 1)
    gate_vals = jnp.swapaxes(got_gate.astype(jnp.float32), 0, 1)
    beta_vals = jnp.swapaxes(got_beta.astype(jnp.float32), 0, 1)
    local_out, reach, slab_map, slab_state = slab_local(
        queries, keys_in, values, gate_vals, beta_vals
    )

    def advance(counter, carried):
        return shifted(product(slab_map, carried) + slab_state, "seq", 1)

    incoming = lax.fori_loop(0, lax.axis_size("seq") - 1, advance, jnp.zeros_like(slab_state))
    combined = local_out + product(reach, incoming)
    head_rows = jnp.swapaxes(combined, 0, 1).astype(jnp.bfloat16)
    flat_rows = head_rows.reshape(head_rows.shape[0], -1)
    head_output = lax.all_to_all(flat_rows, "head", split_axis=0, concat_axis=1, tiled=True)
    last_state = (product(slab_map, incoming) + slab_state)[None]
    return (head_output, last_state)


def solution(mesh):
    return jax.shard_map(
        per_device,
        mesh=mesh,
        in_specs=(
            P(("seq", "head"), None, None),
            P(("seq", "head"), None, None),
            P(("seq", "head"), None, None),
            P(("seq", "head"), None),
            P(("seq", "head"), None),
        ),
        out_specs=(P(("seq", "head"), None), P("seq", "head", None, None)),
        check_vma=False,
    )
```

profile of v0, /device:TPU:1, one launch (start us, length us, event | category | flops | bytes accessed | tf_op | source)
XLA Modules:
  0.0 137.4 jit_solution(2216241430026005763)
XLA Ops:
  0.6 1.4 %copy.41 = bf16[16,32]{0,1:T(8,128)(2,1)} copy(bf16[16,32]{1,0:T(8,128)(2,1)} %param.10) | data formatting | bytes 2048 | tf_op args[3]
  2.0 6.4 %all-to-all-start = ((bf16[16,8,4]{0,2,1:T(4,128)(2,1)}), bf16[16,8,4]{0,2,1:T(4,128)(2,1)S(1)}, u32[]{:S(2)}, u32[]{:S(2)}) async-start(bf16[16,8,4]{0,2,1:T(4,128)(2,1)} %bitcast), calls=%async_computation | async-start | bytes 16384 | tf_op jit(solution)/shard_map/all_to_all | solution.py:112
  10.8 2.9 %all-to-all-done = bf16[16,8,4]{0,2,1:T(4,128)(2,1)S(1)} async-done(((bf16[16,8,4]{0,2,1:T(4,128)(2,1)}), bf16[16,8,4]{0,2,1:T(4,128)(2,1)S(1)}, u32[]{:S(2)}, u32[]{:S(2)}) %all-to-all-start) | async-done | bytes 1056 | tf_op jit(solution)/shard_map/all_to_all | solution.py:112
  13.8 3.3 %all-to-all-start.3 = ((bf16[16,8,4]{0,2,1:T(4,128)(2,1)}), bf16[16,8,4]{0,2,1:T(4,128)(2,1)S(1)}, u32[]{:S(2)}, u32[]{:S(2)}) async-start(bf16[16,8,4]{0,2,1:T(4,128)(2,1)} %bitcast.19), calls=%async_computation.3 | async-start | bytes 16384 | tf_op jit(solution)/shard_map/all_to_all | solution.py:113
  17.3 0.9 reduce_window_sum.11
  18.4 4.0 %all-to-all-done.3 = bf16[16,8,4]{0,2,1:T(4,128)(2,1)S(1)} async-done(((bf16[16,8,4]{0,2,1:T(4,128)(2,1)}), bf16[16,8,4]{0,2,1:T(4,128)(2,1)S(1)}, u32[]{:S(2)}, u32[]{:S(2)}) %all-to-all-start.3) | async-done | bytes 1056 | tf_op jit(solution)/shard_map/all_to_all | solution.py:113
  22.4 3.4 %all-to-all-start.4 = ((bf16[16,32,128]{2,0,1:T(8,128)(2,1)}), bf16[16,32,128]{2,0,1:T(8,128)(2,1)S(1)}, u32[]{:S(2)}, u32[]{:S(2)}) async-start(bf16[16,32,128]{2,0,1:T(8,128)(2,1)} %copy.51), calls=%async_computation.4 | async-start | bytes 262144 | tf_op jit(solution)/shard_map/all_to_all | solution.py:111
  26.3 5.7 %all-to-all-done.4 = bf16[16,32,128]{2,0,1:T(8,128)(2,1)S(1)} async-done(((bf16[16,32,128]{2,0,1:T(8,128)(2,1)}), bf16[16,32,128]{2,0,1:T(8,128)(2,1)S(1)}, u32[]{:S(2)}, u32[]{:S(2)}) %all-to-all-start.4) | async-done | bytes 131104 | tf_op jit(solution)/shard_map/all_to_all | solution.py:111
  32.6 3.4 %all-to-all-start.2 = ((bf16[16,32,128]{2,0,1:T(8,128)(2,1)}), bf16[16,32,128]{2,0,1:T(8,128)(2,1)S(1)}, u32[]{:S(2)}, u32[]{:S(2)}) async-start(bf16[16,32,128]{2,0,1:T(8,128)(2,1)} %bitcast.11), calls=%async_computation.2 | async-start | bytes 262144 | tf_op jit(solution)/shard_map/all_to_all | solution.py:108
  36.0 6.1 %all-to-all-done.2 = bf16[16,32,128]{2,0,1:T(8,128)(2,1)S(1)} async-done(((bf16[16,32,128]{2,0,1:T(8,128)(2,1)}), bf16[16,32,128]{2,0,1:T(8,128)(2,1)S(1)}, u32[]{:S(2)}, u32[]{:S(2)}) %all-to-all-start.2) | async-done | bytes 131104 | tf_op jit(solution)/shard_map/all_to_all | solution.py:108
  42.8 3.4 %all-to-all-start.1 = ((bf16[16,32,128]{2,0,1:T(8,128)(2,1)}), bf16[16,32,128]{2,0,1:T(8,128)(2,1)S(1)}, u32[]{:S(2)}, u32[]{:S(2)}) async-start(bf16[16,32,128]{2,0,1:T(8,128)(2,1)} %bitcast.3), calls=%async_computation.1 | async-start | bytes 262144 | tf_op jit(solution)/shard_map/all_to_all | solution.py:101
  47.2 39.3 %custom-call.4 = f32[4,2,1,64,64]{3,4,2,1,0:T(8,128)S(1)} custom-call(f32[4,2,1,64,64]{4,3,2,1,0:T(8,128)S(1)} %fusion.6), custom_call_target="InvertDiagBlocksLowerTriangular" | custom-call | tf_op jit(solution)/shard_map/jit(_solve_triangular)/vmap(vmap())/triangular_solve | solution.py:42
  87.4 1.1 fusion.31
  88.5 1.1 convolution_subtract_fusion
  95.2 28.5 %while.10 = (s32[]{:T(128)}, f32[4,128,128]{2,1,0:T(8,128)S(1)}, f32[4,128,128]{2,1,0:T(8,128)S(1)}, f32[4,128,128]{2,1,0:T(8,128)S(1)}, s32[]{:T(128)}) while((s32[]{:T(128)}, f32[4,128,128]{2,1,0:T(8,128)S(1)}, f32[4,128,128]{2,1,0:T(8,128)S(1)}, f32[4,128,128]{2,1,0:T(8,128)S(1)}, s32[]{:T(128)}) %tuple.27), condition=%wide.region_4.5_spmd, body=%wide.region_3.4_spmd.sunk | while | flops 100728832 | bytes 2097253 | solution.py:127
  95.7 8.6 %collective-permute-start = (f32[4,128,128]{2,1,0:T(8,128)S(1)}, f32[4,128,128]{2,1,0:T(8,128)S(1)}, u32[]{:S(2)}, u32[]{:S(2)}) collective-permute-start(f32[4,128,128]{2,1,0:T(8,128)S(1)} %convolution_add_fusion.4), channel_id=1, source_target_pairs={{0,8},{8,16},{16,24},{1,9},{9,17},{17,25},{2,10},{10,18},{18,26},{... | collective-permute-start | bytes 786440 | tf_op jit(solution)/shard_map/while/body/eval_jaxpr/ppermute | solution.py:15
  104.2 3.3 %collective-permute-done = f32[4,128,128]{2,1,0:T(8,128)S(1)} collective-permute-done((f32[4,128,128]{2,1,0:T(8,128)S(1)}, f32[4,128,128]{2,1,0:T(8,128)S(1)}, u32[]{:S(2)}, u32[]{:S(2)}) %collective-permute-start) | collective-permute-done | bytes 262176 | tf_op jit(solution)/shard_map/while/body/eval_jaxpr/ppermute | solution.py:15
  107.9 4.4 %collective-permute-start = (f32[4,128,128]{2,1,0:T(8,128)S(1)}, f32[4,128,128]{2,1,0:T(8,128)S(1)}, u32[]{:S(2)}, u32[]{:S(2)}) collective-permute-start(f32[4,128,128]{2,1,0:T(8,128)S(1)} %convolution_add_fusion.4), channel_id=1, source_target_pairs={{0,8},{8,16},{16,24},{1,9},{9,17},{17,25},{2,10},{10,18},{18,26},{... | collective-permute-start | bytes 786440 | tf_op jit(solution)/shard_map/while/body/eval_jaxpr/ppermute | solution.py:15
  112.3 3.3 %collective-permute-done = f32[4,128,128]{2,1,0:T(8,128)S(1)} collective-permute-done((f32[4,128,128]{2,1,0:T(8,128)S(1)}, f32[4,128,128]{2,1,0:T(8,128)S(1)}, u32[]{:S(2)}, u32[]{:S(2)}) %collective-permute-start) | collective-permute-done | bytes 262176 | tf_op jit(solution)/shard_map/while/body/eval_jaxpr/ppermute | solution.py:15
  116.0 4.4 %collective-permute-start = (f32[4,128,128]{2,1,0:T(8,128)S(1)}, f32[4,128,128]{2,1,0:T(8,128)S(1)}, u32[]{:S(2)}, u32[]{:S(2)}) collective-permute-start(f32[4,128,128]{2,1,0:T(8,128)S(1)} %convolution_add_fusion.4), channel_id=1, source_target_pairs={{0,8},{8,16},{16,24},{1,9},{9,17},{17,25},{2,10},{10,18},{18,26},{... | collective-permute-start | bytes 786440 | tf_op jit(solution)/shard_map/while/body/eval_jaxpr/ppermute | solution.py:15
  120.4 3.3 %collective-permute-done = f32[4,128,128]{2,1,0:T(8,128)S(1)} collective-permute-done((f32[4,128,128]{2,1,0:T(8,128)S(1)}, f32[4,128,128]{2,1,0:T(8,128)S(1)}, u32[]{:S(2)}, u32[]{:S(2)}) %collective-permute-start) | collective-permute-done | bytes 262176 | tf_op jit(solution)/shard_map/while/body/eval_jaxpr/ppermute | solution.py:15
  124.9 5.6 %all-to-all-start.5 = ((bf16[8,16,512]{2,1,0:T(8,128)(2,1)}), bf16[8,16,512]{2,1,0:T(8,128)(2,1)S(1)}, u32[]{:S(2)}, u32[]{:S(2)}) async-start(bf16[8,16,512]{2,1,0:T(8,128)(2,1)} %all_to_all.62), calls=%async_computation.5 | async-start | bytes 262144 | tf_op jit(solution)/shard_map/all_to_all | solution.py:131
  130.6 1.1 fusion
  131.7 5.1 %all-to-all-done.5 = bf16[8,16,512]{2,1,0:T(8,128)(2,1)S(1)} async-done(((bf16[8,16,512]{2,1,0:T(8,128)(2,1)}), bf16[8,16,512]{2,1,0:T(8,128)(2,1)S(1)}, u32[]{:S(2)}, u32[]{:S(2)}) %all-to-all-start.5) | async-done | bytes 131104 | tf_op jit(solution)/shard_map/all_to_all | solution.py:131
  (82 shorter events, 14.9 us)
Async XLA Ops:
  0.6 7.9 %copy-start.2 = (bf16[16,32,128]{2,1,0:T(8,128)(2,1)S(1)}, bf16[16,32,128]{2,1,0:T(8,128)(2,1)}, u32[]{:S(2)}) copy-start(bf16[16,32,128]{2,1,0:T(8,128)(2,1)} %param.9) | copy-start | bytes 393220
  2.0 11.8 %all-to-all-start = ((bf16[16,8,4]{0,2,1:T(4,128)(2,1)}), bf16[16,8,4]{0,2,1:T(4,128)(2,1)S(1)}, u32[]{:S(2)}, u32[]{:S(2)}) async-start(bf16[16,8,4]{0,2,1:T(4,128)(2,1)} %bitcast), calls=%async_computation | async-start | bytes 16384 | tf_op jit(solution)/shard_map/all_to_all | solution.py:112
  8.6 0.7 copy-start.5
  8.6 1.4 %copy-start.3 = (bf16[16,16,128]{2,1,0:T(8,128)(2,1)S(1)}, bf16[16,16,128]{2,1,0:T(8,128)(2,1)}, u32[]{:S(2)}) copy-start(bf16[16,16,128]{2,1,0:T(8,128)(2,1)} %param.8) | copy-start | bytes 196612
  10.0 0.8 copy-start.4
  13.8 8.6 %all-to-all-start.3 = ((bf16[16,8,4]{0,2,1:T(4,128)(2,1)}), bf16[16,8,4]{0,2,1:T(4,128)(2,1)S(1)}, u32[]{:S(2)}, u32[]{:S(2)}) async-start(bf16[16,8,4]{0,2,1:T(4,128)(2,1)} %bitcast.19), calls=%async_computation.3 | async-start | bytes 16384 | tf_op jit(solution)/shard_map/all_to_all | solution.py:113
  22.4 9.5 %all-to-all-start.4 = ((bf16[16,32,128]{2,0,1:T(8,128)(2,1)}), bf16[16,32,128]{2,0,1:T(8,128)(2,1)S(1)}, u32[]{:S(2)}, u32[]{:S(2)}) async-start(bf16[16,32,128]{2,0,1:T(8,128)(2,1)} %copy.51), calls=%async_computation.4 | async-start | bytes 262144 | tf_op jit(solution)/shard_map/all_to_all | solution.py:111
  32.6 9.5 %all-to-all-start.2 = ((bf16[16,32,128]{2,0,1:T(8,128)(2,1)}), bf16[16,32,128]{2,0,1:T(8,128)(2,1)S(1)}, u32[]{:S(2)}, u32[]{:S(2)}) async-start(bf16[16,32,128]{2,0,1:T(8,128)(2,1)} %bitcast.11), calls=%async_computation.2 | async-start | bytes 262144 | tf_op jit(solution)/shard_map/all_to_all | solution.py:108
  42.8 47.7 %all-to-all-start.1 = ((bf16[16,32,128]{2,0,1:T(8,128)(2,1)}), bf16[16,32,128]{2,0,1:T(8,128)(2,1)S(1)}, u32[]{:S(2)}, u32[]{:S(2)}) async-start(bf16[16,32,128]{2,0,1:T(8,128)(2,1)} %bitcast.3), calls=%async_computation.1 | async-start | bytes 262144 | tf_op jit(solution)/shard_map/all_to_all | solution.py:101
  91.9 0.8 copy-start.1
  92.3 0.7 copy-start
  93.4 0.9 slice-start.1
  94.3 0.9 slice-start
  95.7 11.9 %collective-permute-start = (f32[4,128,128]{2,1,0:T(8,128)S(1)}, f32[4,128,128]{2,1,0:T(8,128)S(1)}, u32[]{:S(2)}, u32[]{:S(2)}) collective-permute-start(f32[4,128,128]{2,1,0:T(8,128)S(1)} %convolution_add_fusion.4), channel_id=1, source_target_pairs={{0,8},{8,16},{16,24},{1,9},{9,17},{17,25},{2,10},{10,18},{18,26},{... | collective-permute-start | bytes 786440 | tf_op jit(solution)/shard_map/while/body/eval_jaxpr/ppermute | solution.py:15
  107.9 7.7 %collective-permute-start = (f32[4,128,128]{2,1,0:T(8,128)S(1)}, f32[4,128,128]{2,1,0:T(8,128)S(1)}, u32[]{:S(2)}, u32[]{:S(2)}) collective-permute-start(f32[4,128,128]{2,1,0:T(8,128)S(1)} %convolution_add_fusion.4), channel_id=1, source_target_pairs={{0,8},{8,16},{16,24},{1,9},{9,17},{17,25},{2,10},{10,18},{18,26},{... | collective-permute-start | bytes 786440 | tf_op jit(solution)/shard_map/while/body/eval_jaxpr/ppermute | solution.py:15
  116.0 7.7 %collective-permute-start = (f32[4,128,128]{2,1,0:T(8,128)S(1)}, f32[4,128,128]{2,1,0:T(8,128)S(1)}, u32[]{:S(2)}, u32[]{:S(2)}) collective-permute-start(f32[4,128,128]{2,1,0:T(8,128)S(1)} %convolution_add_fusion.4), channel_id=1, source_target_pairs={{0,8},{8,16},{16,24},{1,9},{9,17},{17,25},{2,10},{10,18},{18,26},{... | collective-permute-start | bytes 786440 | tf_op jit(solution)/shard_map/while/body/eval_jaxpr/ppermute | solution.py:15
  124.9 11.8 %all-to-all-start.5 = ((bf16[8,16,512]{2,1,0:T(8,128)(2,1)}), bf16[8,16,512]{2,1,0:T(8,128)(2,1)S(1)}, u32[]{:S(2)}, u32[]{:S(2)}) async-start(bf16[8,16,512]{2,1,0:T(8,128)(2,1)} %all_to_all.62), calls=%async_computation.5 | async-start | bytes 262144 | tf_op jit(solution)/shard_map/all_to_all | solution.py:131
where the time goes:
time: 140 us; the launch traced here: 137 us
  starting transfers between devices  42.8 us (31%)
  other arithmetic  41.4 us (30%)
  waiting for transfers between devices  33.7 us (24%)
  local copies, waits for them, and re-layouts  9.5 us (7%)
  matrix products  8.91 us (6%)
    another operation x2, other arithmetic, stretch_parts(): jax.scipy.linalg.solve_triangular(identity + lower_triangle, right_side,...  39.3 us
    ppermute x3, starting transfers between devices, shifted(): return lax.ppermute(block, axis, route)  17.3 us
    ppermute x3, waiting for transfers between devices, shifted(): return lax.ppermute(block, axis, route)  9.87 us
    all_to_all x1, starting transfers between devices, per_device(): lax.all_to_all(gate_log, 'head', split_axis=1, concat_axis=0, tiled=True)  6.38 us
    all_to_all x1, waiting for transfers between devices, per_device(): lax.all_to_all(jnp.repeat(key_heads, grouping, axis=1), 'head', split_axi...  6.08 us
    all_to_all x1, waiting for transfers between devices, per_device(): lax.all_to_all(value_heads, 'head', split_axis=1, concat_axis=0, tiled=True)  5.67 us
    all_to_all x1, starting transfers between devices, per_device(): lax.all_to_all(flat_rows, 'head', split_axis=0, concat_axis=1, tiled=True)  5.65 us
    all_to_all x1, waiting for transfers between devices, per_device(): lax.all_to_all(flat_rows, 'head', split_axis=0, concat_axis=1, tiled=True)  5.1 us
  transfers between devices with their start and end apart: 9, of which 8 were waited for; matrix products, arithmetic and copies ran while one was open for 35% of the time, Pallas kernels for 0%

commit v1 on v0

--- a/solution.py
+++ b/solution.py
@@ -1,9 +1,14 @@
+import functools
+
 import jax
 import jax.numpy as jnp
 from jax import lax
+from jax.experimental import pallas as pl
+from jax.experimental.pallas import tpu as pltpu
 from jax.sharding import PartitionSpec as P
 
 STRETCH = 64
+MESH = pl.DeviceIdType.MESH
 
 
 HIGHEST = lax.Precision.HIGHEST
@@ -133,9 +138,325 @@
     return (head_output, last_state)
 
 
+def split(matrix):
+    high = matrix.astype(jnp.bfloat16)
+    low = (matrix - high.astype(jnp.float32)).astype(jnp.bfloat16)
+    return high, low
+
+
+def dot(left, right):
+    return jnp.dot(left, right, preferred_element_type=jnp.float32)
+
+
+def wide(matrix):
+    return jnp.concatenate(split(matrix), axis=1)
+
+
+def tall(*matrices):
+    row = jnp.concatenate([half for matrix in matrices for half in split(matrix)], axis=1)
+    return jnp.concatenate([row, row], axis=0)
+
+
+def fold(product):
+    width = product.shape[1] // 2
+    return product[:, :width] + product[:, width:]
+
+
+def mul(left, right):
+    return fold(dot(wide(left), tall(right)))
+
+
+def fast_kernel(
+    sizes,
+    q_hbm,
+    k_hbm,
+    v_hbm,
+    g_hbm,
+    b_hbm,
+    out_ref,
+    states_ref,
+    q_in,
+    k_in,
+    v_in,
+    g_in,
+    b_in,
+    q_wide,
+    k_wide,
+    v_wide,
+    send,
+    gb_send,
+    recv,
+    gb_recv,
+    out_buf,
+    state_buf,
+    load_sem,
+    send_sem,
+    recv_sem,
+):
+    ns, nh, tokens, heads, grouping = sizes
+    key_heads = heads // grouping
+    slab = nh * tokens
+    width = 128
+    s = lax.axis_index("seq")
+    h = lax.axis_index("head")
+    mine = h * ns + s
+
+    loads = [
+        pltpu.make_async_copy(source, target, load_sem.at[i])
+        for i, (source, target) in enumerate(
+            [(q_hbm, q_in), (k_hbm, k_in), (v_hbm, v_in), (g_hbm, g_in), (b_hbm, b_in)]
+        )
+    ]
+    for load in loads:
+        load.start()
+
+    peers = []
+    for ds in range(ns):
+        for dh in range(nh):
+            peers.append((lax.rem(s + ds, ns), lax.rem(h + dh, nh)))
+
+    barrier = pltpu.get_barrier_semaphore()
+    for ps, ph in peers[1:]:
+        pl.semaphore_signal(barrier, inc=1, device_id=(ps, ph), device_id_type=MESH)
+
+    for load in loads:
+        load.wait()
+    q_wide[...] = q_in[...].astype(jnp.float32).reshape(tokens * key_heads, width)
+    k_wide[...] = k_in[...].astype(jnp.float32).reshape(tokens * key_heads, width)
+    v_wide[...] = v_in[...].astype(jnp.float32).reshape(tokens * heads, width)
+    for j in range(key_heads):
+        queries = q_wide[pl.ds(j, tokens, stride=key_heads), :].astype(jnp.bfloat16)
+        keys = k_wide[pl.ds(j, tokens, stride=key_heads), :].astype(jnp.bfloat16)
+        for g in range(grouping):
+            send[j * grouping + g, 0:tokens, :] = queries
+            send[j * grouping + g, tokens : 2 * tokens, :] = keys
+    for j in range(heads):
+        values = v_wide[pl.ds(j, tokens, stride=heads), :].astype(jnp.bfloat16)
+        send[j, 2 * tokens : 3 * tokens, :] = values
+    both = jnp.concatenate([g_in[...], b_in[...]], axis=0).astype(jnp.float32)
+    place_row = lax.broadcasted_iota(jnp.int32, (2 * tokens, width), 0)
+    place_col = lax.broadcasted_iota(jnp.int32, (2 * tokens, width), 1)
+    place = (place_row == place_col).astype(jnp.bfloat16)
+    turned = dot(both.T.astype(jnp.bfloat16), place)
+    for j in range(heads):
+        gb_send[j, :, :] = turned[j : j + 1, :]
+
+    pl.semaphore_wait(barrier, ns * nh - 1)
+
+    for i, (ps, ph) in enumerate(peers):
+        j = ph * ns + ps
+        if i == 0:
+            pltpu.make_async_copy(send.at[j], recv.at[s, h], recv_sem.at[0]).start()
+            pltpu.make_async_copy(gb_send.at[j], gb_recv.at[s, h], recv_sem.at[1]).start()
+        else:
+            for source, target, n in ((gb_send, gb_recv, 1), (send, recv, 0)):
+                pltpu.make_async_remote_copy(
+                    src_ref=source.at[j],
+                    dst_ref=target.at[s, h],
+                    send_sem=send_sem.at[n],
+                    recv_sem=recv_sem.at[n],
+                    device_id=(ps, ph),
+                    device_id_type=MESH,
+                ).start()
+
+    row_ids = lax.broadcasted_iota(jnp.int32, (slab, slab), 0)
+    col_ids = lax.broadcasted_iota(jnp.int32, (slab, slab), 1)
+    strict = row_ids > col_ids
+    inclusive = row_ids >= col_ids
+    eye = (row_ids == col_ids).astype(jnp.float32)
+    lower_ones = inclusive.astype(jnp.bfloat16)
+    all_ones = jnp.ones((slab, slab), jnp.bfloat16)
+    token_at = row_ids % tokens
+    expand = (
+        lax.broadcasted_iota(jnp.int32, (slab, nh), 0) // tokens
+        == lax.broadcasted_iota(jnp.int32, (slab, nh), 1)
+    ).astype(jnp.bfloat16)
+
+    pltpu.make_async_copy(gb_recv, gb_recv, recv_sem.at[1]).wait()
+    cums, betas = [], []
+    for n in range(ns):
+        rates = dot(expand, gb_recv[n, :, 0, :].astype(jnp.bfloat16))
+        gates = jnp.where(col_ids == token_at, rates, 0.0).astype(jnp.bfloat16)
+        writes = jnp.where(col_ids == token_at + tokens, rates, 0.0).astype(jnp.bfloat16)
+        gate_cols = dot(gates, all_ones).astype(jnp.bfloat16)
+        cums.append(dot(lower_ones, gate_cols))
+        betas.append(dot(writes, all_ones))
+
+    pltpu.make_async_copy(recv, recv, recv_sem.at[0]).wait()
+
+    parts = []
+    for n in range(ns):
+        queries = recv[n, :, 0:tokens, :].reshape(slab, width)
+        keys = recv[n, :, tokens : 2 * tokens, :].reshape(slab, width)
+        values = recv[n, :, 2 * tokens : 3 * tokens, :].reshape(slab, width)
+        cum, beta = cums[n], betas[n]
+        q32, k32 = queries.astype(jnp.float32), keys.astype(jnp.float32)
+        q_norm = 1.0 / jnp.sqrt(jnp.sum(q32 * q32, axis=1, keepdims=True) + 1e-06)
+        k_norm = 1.0 / jnp.sqrt(jnp.sum(k32 * k32, axis=1, keepdims=True) + 1e-06)
+        columns = jnp.where(col_ids == 0, cum, jnp.where(col_ids == 1, k_norm, beta))
+        rows = columns.T
+        cum_row, k_norm_row, beta_row = rows[0:1, :], rows[1:2, :], rows[2:3, :]
+        k_turned = k32.T.astype(jnp.bfloat16)
+        decay = jnp.where(inclusive, jnp.exp(jnp.where(inclusive, cum - cum_row, 0.0)), 0.0)
+        decay = decay * k_norm_row
+        key_key = dot(keys, k_turned)
+        query_key = dot(queries, k_turned)
+        lower = jnp.where(strict, (beta * k_norm) * decay * key_key, 0.0)
+        scores = q_norm * decay * query_key
+        parts.append((queries, keys, values, cum, k_norm, q_norm, cum_row, k_norm_row, beta_row,
+                      k_turned, lower, scores, q32))
+
+    small = 32
+    same = (row_ids // small) == (col_ids // small)
+    lowers = [part[10] for part in parts]
+    blocks = [jnp.where(same, lower, 0.0) for lower in lowers]
+    inverses = [eye - block for block in blocks]
+    powers = [mul(block, block) for block in blocks]
+    reach = 2
+    while reach < small:
+        last = reach * 2 >= small
+        for n in range(ns):
+            right = tall(powers[n])
+            if last:
+                inverses[n] = inverses[n] + fold(dot(wide(inverses[n]), right))
+            else:
+                left = jnp.concatenate([wide(inverses[n]), wide(powers[n])], axis=0)
+                both_products = fold(dot(left, right))
+                inverses[n] = inverses[n] + both_products[:slab]
+                powers[n] = both_products[slab:]
+        reach *= 2
+    size = small
+    while size < slab:
+        pair = ((row_ids // (2 * size)) == (col_ids // (2 * size))) & (
+            (row_ids // size) != (col_ids // size)
+        )
+        inner = [mul(jnp.where(pair, lowers[n], 0.0), inverses[n]) for n in range(ns)]
+        inverses = [inverses[n] - mul(inverses[n], inner[n]) for n in range(ns)]
+        size *= 2
+
+    maps = []
+    for n in range(ns):
+        (queries, keys, values, cum, k_norm, q_norm, cum_row, k_norm_row, beta_row,
+         k_turned, lower, scores, q32) = parts[n]
+        solve = inverses[n] * beta_row
+        write_vals = dot(wide(solve), jnp.concatenate([values, values], axis=0))
+        final = cum[slab - 1 : slab, :]
+        key_decay = jnp.exp(final - cum) * k_norm
+        if n == 0:
+            inject = fold(dot(k_turned, wide(key_decay * write_vals)))
+            direct = mul(scores, write_vals)
+            maps.append((None, None, inject, direct, None))
+            continue
+        key_solve = solve * (jnp.exp(cum_row) * k_norm_row)
+        write_keys = dot(wide(key_solve), jnp.concatenate([keys, keys], axis=0))
+        scaled = jnp.concatenate([wide(key_decay * write_keys), wide(key_decay * write_vals)], axis=1)
+        moved = dot(k_turned, scaled)
+        read = dot(wide(scores), tall(write_keys, write_vals))
+        project = (jnp.exp(cum) * q_norm) * q32 - fold(read[:, : 2 * width])
+        maps.append((fold(moved[:, : 2 * width]), project, fold(moved[:, 2 * width :]),
+                     fold(read[:, 2 * width :]), jnp.exp(final)))
+
+    state = None
+    for n in range(ns):
+        erase, project, inject, direct, total_decay = maps[n]
+        if n == 0:
+            output, state = direct, inject
+        else:
+            right = tall(state)
+            products = fold(dot(jnp.concatenate([wide(erase), wide(project)], axis=0), right))
+            output = direct + products[slab:]
+            state = total_decay * state + inject - products[:slab]
+        out_buf[n * nh : (n + 1) * nh] = output.astype(jnp.bfloat16).reshape(nh, tokens, width)
+        state_buf[n] = state
+
+    columns = pl.ds(pl.multiple_of(mine * width, width), width)
+    for i, (ps, ph) in enumerate(peers):
+        block = out_buf.at[ps * nh + ph]
+        target = out_ref.at[:, columns]
+        if i == 0:
+            pltpu.make_async_copy(block, target, recv_sem.at[2]).start()
+            pltpu.make_async_copy(state_buf.at[s], states_ref.at[0, s], recv_sem.at[3]).start()
+        else:
+            pltpu.make_async_remote_copy(
+                src_ref=block,
+                dst_ref=target,
+                send_sem=send_sem.at[2],
+                recv_sem=recv_sem.at[2],
+                device_id=(ps, ph),
+                device_id_type=MESH,
+            ).start()
+        if i > 0 and i % nh == 0:
+            pltpu.make_async_remote_copy(
+                src_ref=state_buf.at[ps],
+                dst_ref=states_ref.at[0, s],
+                send_sem=send_sem.at[3],
+                recv_sem=recv_sem.at[3],
+                device_id=(ps, h),
+                device_id_type=MESH,
+            ).start()
+
+    others = pl.ds(0, ns * nh - 1)
+    pltpu.make_async_copy(send.at[others], send.at[others], send_sem.at[0]).wait()
+    pltpu.make_async_copy(gb_send.at[others], gb_send.at[others], send_sem.at[1]).wait()
+    pltpu.make_async_copy(out_buf.at[others], out_buf.at[others], send_sem.at[2]).wait()
+    rest = state_buf.at[pl.ds(0, ns - 1)]
+    pltpu.make_async_copy(rest, rest, send_sem.at[3]).wait()
+    pltpu.make_async_copy(out_ref, out_ref, recv_sem.at[2]).wait()
+    pltpu.make_async_copy(states_ref, states_ref, recv_sem.at[3]).wait()
+
+
+def fast_device(query_heads, key_heads, value_heads, gate_log, beta_rate):
+    ns, nh = lax.axis_size("seq"), lax.axis_size("head")
+    tokens, heads, width = value_heads.shape
+    key_count = key_heads.shape[1]
+    sizes = (ns, nh, tokens, heads, heads // key_count)
+    bf16, f32 = jnp.bfloat16, jnp.float32
+    vmem = pl.BlockSpec(memory_space=pltpu.VMEM)
+    return pl.pallas_call(
+        functools.partial(fast_kernel, sizes),
+        out_shape=(
+            jax.ShapeDtypeStruct((tokens, heads * width), bf16),
+            jax.ShapeDtypeStruct((1, ns, width, width), f32),
+        ),
+        in_specs=[pl.BlockSpec(memory_space=pl.ANY)] * 5,
+        out_specs=(vmem, vmem),
+        scratch_shapes=[
+            pltpu.VMEM((tokens, key_count, width), bf16),
+            pltpu.VMEM((tokens, key_count, width), bf16),
+            pltpu.VMEM((tokens, heads, width), bf16),
+            pltpu.VMEM((tokens, heads), bf16),
+            pltpu.VMEM((tokens, heads), bf16),
+            pltpu.VMEM((tokens * key_count, width), f32),
+            pltpu.VMEM((tokens * key_count, width), f32),
+            pltpu.VMEM((tokens * heads, width), f32),
+            pltpu.VMEM((heads, 3 * tokens, width), bf16),
+            pltpu.VMEM((heads, 1, width), f32),
+            pltpu.VMEM((ns, nh, 3 * tokens, width), bf16),
+            pltpu.VMEM((ns, nh, 1, width), f32),
+            pltpu.VMEM((ns * nh, tokens, width), bf16),
+            pltpu.VMEM((ns, width, width), f32),
+            pltpu.SemaphoreType.DMA((5,)),
+            pltpu.SemaphoreType.DMA((4,)),
+            pltpu.SemaphoreType.DMA((4,)),
+        ],
+        compiler_params=pltpu.CompilerParams(
+            collective_id=0, has_side_effects=True, vmem_limit_bytes=32 * 1024 * 1024
+        ),
+    )(query_heads, key_heads, value_heads, gate_log, beta_rate)
+
+
+def choose_device(query_heads, key_heads, value_heads, gate_log, beta_rate):
+    ns, nh = lax.axis_size("seq"), lax.axis_size("head")
+    tokens, heads, width = value_heads.shape
+    fits = ns * nh == heads and tokens == 16 and nh * tokens == 128
+    fits = fits and width == 128 and key_heads.shape[2] == 128
+    run = fast_device if fits else per_device
+    return run(query_heads, key_heads, value_heads, gate_log, beta_rate)
+
+
 def solution(mesh):
     return jax.shard_map(
-        per_device,
+        choose_device,
         mesh=mesh,
         in_specs=(
             P(("seq", "head"), None, None),

time: 140 us -> 34.9 us (0.25); the launches traced: 137 us -> 34.5 us
  starting transfers between devices: 42.8 us -> 0 us
  other arithmetic: 41.4 us -> 0 us
  waiting for transfers between devices: 33.7 us -> 0 us
  Pallas kernels: 0 us -> 28.5 us
  matrix products: 8.91 us -> 0 us
  local copies, waits for them, and re-layouts: 9.5 us -> 5.31 us
    another operation x3 -> x0, other arithmetic: 40.3 us -> none  [the longest x2 39.3 us: stretch_parts(): jax.scipy.linalg.solve_triangular(identity + lower_triangle, right_side,...]
    pallas_call x0 -> x1, Pallas kernels: none -> 28.5 us  [fast_device(): pl.pallas_call(functools.partial(fast_kernel, sizes), out_shape=(jax.Shap...]
    all_to_all x6 -> x0, starting transfers between devices: 25.5 us -> none  [the longest x1 6.38 us: per_device(): lax.all_to_all(gate_log, 'head', split_axis=1, concat_axis=0, tiled=True)]
    all_to_all x6 -> x0, waiting for transfers between devices: 23.8 us -> none  [the longest x1 6.08 us: per_device(): lax.all_to_all(jnp.repeat(key_heads, grouping, axis=1), 'head', split_axi...]
    ppermute x3 -> x0, starting transfers between devices: 17.3 us -> none  [shifted(): return lax.ppermute(block, axis, route)]
    ppermute x3 -> x0, waiting for transfers between devices: 9.87 us -> none  [shifted(): return lax.ppermute(block, axis, route)]
    dot_general x15 -> x0, matrix products: 8.27 us -> none  [the longest x9 4.17 us: product(): jnp.einsum('...ij,...jk->...ik', left_mat, right_mat, precision=HIGHEST)]
    slice x8 -> x0, local copies, waits for them, and re-layouts: 1.96 us -> none  [the longest x2 0.88 us: slab_local(): project[:, :1]]
  transfers between devices with their start and end apart: 9 -> 0, of which waited for: 8 -> 0; matrix products, arithmetic and copies ran while one was open for 35% -> 0% of each run, Pallas kernels for 0% -> 0%
where the time goes in v1:
time: 34.9 us; the launch traced here: 34.5 us
  Pallas kernels  28.5 us (82%)
  local copies, waits for them, and re-layouts  5.31 us (15%)
  between operations  0.65 us (2%)
    pallas_call x1, Pallas kernels, fast_device(): pl.pallas_call(functools.partial(fast_kernel, sizes), out_shape=(jax.Shap...  28.5 us
    unnamed x12, local copies, waits for them, and re-layouts  5.31 us

profile of v1, /device:TPU:1, one launch (start us, length us, event | category | flops | bytes accessed | tf_op | source)
XLA Modules:
  0.0 34.5 jit_solution(10575623251128017517)
XLA Ops:
  0.6 0.0 copy-start
  0.6 0.9 %copy-done = bf16[16,32,128]{2,1,0:T(8,128)(2,1)S(1)} copy-done((bf16[16,32,128]{2,1,0:T(8,128)(2,1)S(1)}, bf16[16,32,128]{2,1,0:T(8,128)(2,1)}, u32[]{:S(2)}) %copy-start) | copy-done | bytes 131096
  1.5 0.0 copy-start.1
  1.5 0.8 %copy-done.1 = bf16[16,16,128]{2,1,0:T(8,128)(2,1)S(1)} copy-done((bf16[16,16,128]{2,1,0:T(8,128)(2,1)S(1)}, bf16[16,16,128]{2,1,0:T(8,128)(2,1)}, u32[]{:S(2)}) %copy-start.1) | copy-done | bytes 65560
  2.4 0.0 copy-start.2
  2.4 0.8 %copy-done.2 = bf16[16,16,128]{2,1,0:T(8,128)(2,1)S(1)} copy-done((bf16[16,16,128]{2,1,0:T(8,128)(2,1)S(1)}, bf16[16,16,128]{2,1,0:T(8,128)(2,1)}, u32[]{:S(2)}) %copy-start.2) | copy-done | bytes 65560
  3.2 0.0 copy-start.3
  3.2 0.7 %copy-done.3 = bf16[16,32]{1,0:T(8,128)(2,1)S(1)} copy-done((bf16[16,32]{1,0:T(8,128)(2,1)S(1)}, bf16[16,32]{1,0:T(8,128)(2,1)}, u32[]{:S(2)}) %copy-start.3) | copy-done | bytes 1048
  3.9 0.0 copy-start.4
  3.9 0.7 %copy-done.4 = bf16[16,32]{1,0:T(8,128)(2,1)S(1)} copy-done((bf16[16,32]{1,0:T(8,128)(2,1)S(1)}, bf16[16,32]{1,0:T(8,128)(2,1)}, u32[]{:S(2)}) %copy-start.4) | copy-done | bytes 1048
  4.6 28.5 %shard_map.68 = (bf16[16,4096]{1,0:T(8,128)(2,1)S(1)}, f32[1,4,128,128]{3,2,1,0:T(8,128)S(1)}) custom-call(bf16[16,16,128]{2,1,0:T(8,128)(2,1)S(1)} %copy-done.1, bf16[16,16,128]{2,1,0:T(8,128)(2,1)S(1)} %copy-done.2, bf16[16,32,128]{2,1,0:T(8,128)(2,1)S(1)} %copy-done, bf16[16,32]{1,0:T(8,128)(2,1)S(1)} %copy-done.3, bf16[16,32]{1,0:T(8,128)(2,1)S(1)} %copy-done.4), custom_call_target="tpu_custom_call" | custom-call | tf_op jit(solution)/shard_map/pallas_call | solution.py:415
  33.1 0.7 %copy.9 = bf16[16,4096]{1,0:T(8,128)(2,1)} copy(bf16[16,4096]{1,0:T(8,128)(2,1)S(1)} %get-tuple-element.4) | data formatting | bytes 262144
  33.8 0.7 %copy.10 = f32[1,4,128,128]{3,2,1,0:T(8,128)} copy(f32[1,4,128,128]{3,2,1,0:T(8,128)S(1)} %get-tuple-element.5) | data formatting | bytes 524288
Async XLA Ops:
  0.6 0.9 %copy-start = (bf16[16,32,128]{2,1,0:T(8,128)(2,1)S(1)}, bf16[16,32,128]{2,1,0:T(8,128)(2,1)}, u32[]{:S(2)}) copy-start(bf16[16,32,128]{2,1,0:T(8,128)(2,1)} %v_hbm.1) | copy-start | bytes 393220
  1.5 0.8 %copy-start.1 = (bf16[16,16,128]{2,1,0:T(8,128)(2,1)S(1)}, bf16[16,16,128]{2,1,0:T(8,128)(2,1)}, u32[]{:S(2)}) copy-start(bf16[16,16,128]{2,1,0:T(8,128)(2,1)} %q_hbm.1) | copy-start | bytes 196612
  2.4 0.8 %copy-start.2 = (bf16[16,16,128]{2,1,0:T(8,128)(2,1)S(1)}, bf16[16,16,128]{2,1,0:T(8,128)(2,1)}, u32[]{:S(2)}) copy-start(bf16[16,16,128]{2,1,0:T(8,128)(2,1)} %k_hbm.1) | copy-start | bytes 196612
  3.2 0.7 %copy-start.3 = (bf16[16,32]{1,0:T(8,128)(2,1)S(1)}, bf16[16,32]{1,0:T(8,128)(2,1)}, u32[]{:S(2)}) copy-start(bf16[16,32]{1,0:T(8,128)(2,1)} %g_hbm.1) | copy-start | bytes 3076
  3.9 0.7 %copy-start.4 = (bf16[16,32]{1,0:T(8,128)(2,1)S(1)}, bf16[16,32]{1,0:T(8,128)(2,1)}, u32[]{:S(2)}) copy-start(bf16[16,32]{1,0:T(8,128)(2,1)} %b_hbm.1) | copy-start | bytes 3076

commit v2 on v1

--- a/solution.py
+++ b/solution.py
@@ -189,9 +189,14 @@
     gb_recv,
     out_buf,
     state_buf,
+    step_maps,
+    step_terms,
+    step_decay,
     load_sem,
     send_sem,
     recv_sem,
+    gb_sem,
+    back_sem,
 ):
     ns, nh, tokens, heads, grouping = sizes
     key_heads = heads // grouping
@@ -247,14 +252,14 @@
         j = ph * ns + ps
         if i == 0:
             pltpu.make_async_copy(send.at[j], recv.at[s, h], recv_sem.at[0]).start()
-            pltpu.make_async_copy(gb_send.at[j], gb_recv.at[s, h], recv_sem.at[1]).start()
+            pltpu.make_async_copy(gb_send.at[j], gb_recv.at[s, h], gb_sem.at[0]).start()
         else:
-            for source, target, n in ((gb_send, gb_recv, 1), (send, recv, 0)):
+            for source, target, n, sem in ((gb_send, gb_recv, 1, gb_sem), (send, recv, 0, recv_sem)):
                 pltpu.make_async_remote_copy(
                     src_ref=source.at[j],
                     dst_ref=target.at[s, h],
                     send_sem=send_sem.at[n],
-                    recv_sem=recv_sem.at[n],
+                    recv_sem=sem.at[i // nh],
                     device_id=(ps, ph),
                     device_id_type=MESH,
                 ).start()
@@ -272,128 +277,142 @@
         == lax.broadcasted_iota(jnp.int32, (slab, nh), 1)
     ).astype(jnp.bfloat16)
 
-    pltpu.make_async_copy(gb_recv, gb_recv, recv_sem.at[1]).wait()
-    cums, betas = [], []
-    for n in range(ns):
-        rates = dot(expand, gb_recv[n, :, 0, :].astype(jnp.bfloat16))
-        gates = jnp.where(col_ids == token_at, rates, 0.0).astype(jnp.bfloat16)
-        writes = jnp.where(col_ids == token_at + tokens, rates, 0.0).astype(jnp.bfloat16)
-        gate_cols = dot(gates, all_ones).astype(jnp.bfloat16)
-        cums.append(dot(lower_ones, gate_cols))
-        betas.append(dot(writes, all_ones))
-
-    pltpu.make_async_copy(recv, recv, recv_sem.at[0]).wait()
-
-    parts = []
-    for n in range(ns):
-        queries = recv[n, :, 0:tokens, :].reshape(slab, width)
-        keys = recv[n, :, tokens : 2 * tokens, :].reshape(slab, width)
-        values = recv[n, :, 2 * tokens : 3 * tokens, :].reshape(slab, width)
-        cum, beta = cums[n], betas[n]
-        q32, k32 = queries.astype(jnp.float32), keys.astype(jnp.float32)
-        q_norm = 1.0 / jnp.sqrt(jnp.sum(q32 * q32, axis=1, keepdims=True) + 1e-06)
-        k_norm = 1.0 / jnp.sqrt(jnp.sum(k32 * k32, axis=1, keepdims=True) + 1e-06)
-        columns = jnp.where(col_ids == 0, cum, jnp.where(col_ids == 1, k_norm, beta))
-        rows = columns.T
-        cum_row, k_norm_row, beta_row = rows[0:1, :], rows[1:2, :], rows[2:3, :]
-        k_turned = k32.T.astype(jnp.bfloat16)
-        decay = jnp.where(inclusive, jnp.exp(jnp.where(inclusive, cum - cum_row, 0.0)), 0.0)
-        decay = decay * k_norm_row
-        key_key = dot(keys, k_turned)
-        query_key = dot(queries, k_turned)
-        lower = jnp.where(strict, (beta * k_norm) * decay * key_key, 0.0)
-        scores = q_norm * decay * query_key
-        parts.append((queries, keys, values, cum, k_norm, q_norm, cum_row, k_norm_row, beta_row,
-                      k_turned, lower, scores, q32))
-
-    small = 32
-    same = (row_ids // small) == (col_ids // small)
-    lowers = [part[10] for part in parts]
-    blocks = [jnp.where(same, lower, 0.0) for lower in lowers]
-    inverses = [eye - block for block in blocks]
-    powers = [mul(block, block) for block in blocks]
-    reach = 2
-    while reach < small:
-        last = reach * 2 >= small
-        for n in range(ns):
-            right = tall(powers[n])
-            if last:
-                inverses[n] = inverses[n] + fold(dot(wide(inverses[n]), right))
-            else:
-                left = jnp.concatenate([wide(inverses[n]), wide(powers[n])], axis=0)
-                both_products = fold(dot(left, right))
-                inverses[n] = inverses[n] + both_products[:slab]
-                powers[n] = both_products[slab:]
-        reach *= 2
-    size = small
-    while size < slab:
-        pair = ((row_ids // (2 * size)) == (col_ids // (2 * size))) & (
-            (row_ids // size) != (col_ids // size)
-        )
-        inner = [mul(jnp.where(pair, lowers[n], 0.0), inverses[n]) for n in range(ns)]
-        inverses = [inverses[n] - mul(inverses[n], inner[n]) for n in range(ns)]
-        size *= 2
-
-    maps = []
-    for n in range(ns):
-        (queries, keys, values, cum, k_norm, q_norm, cum_row, k_norm_row, beta_row,
-         k_turned, lower, scores, q32) = parts[n]
-        solve = inverses[n] * beta_row
-        write_vals = dot(wide(solve), jnp.concatenate([values, values], axis=0))
-        final = cum[slab - 1 : slab, :]
-        key_decay = jnp.exp(final - cum) * k_norm
-        if n == 0:
-            inject = fold(dot(k_turned, wide(key_decay * write_vals)))
-            direct = mul(scores, write_vals)
-            maps.append((None, None, inject, direct, None))
-            continue
-        key_solve = solve * (jnp.exp(cum_row) * k_norm_row)
-        write_keys = dot(wide(key_solve), jnp.concatenate([keys, keys], axis=0))
-        scaled = jnp.concatenate([wide(key_decay * write_keys), wide(key_decay * write_vals)], axis=1)
-        moved = dot(k_turned, scaled)
-        read = dot(wide(scores), tall(write_keys, write_vals))
-        project = (jnp.exp(cum) * q_norm) * q32 - fold(read[:, : 2 * width])
-        maps.append((fold(moved[:, : 2 * width]), project, fold(moved[:, 2 * width :]),
-                     fold(read[:, 2 * width :]), jnp.exp(final)))
-
+    for first in range(0, ns, 2):
+        slabs = [lax.rem(s + ns - first - i, ns) for i in range(min(2, ns - first))]
+        count = len(slabs)
+        for i, at in enumerate(slabs):
+            pltpu.make_async_copy(gb_recv.at[at], gb_recv.at[at], gb_sem.at[first + i]).wait()
+        cums, betas = [], []
+        for at in slabs:
+            rates = dot(expand, gb_recv[at, :, 0, :].astype(jnp.bfloat16))
+            gates = jnp.where(col_ids == token_at, rates, 0.0).astype(jnp.bfloat16)
+            writes = jnp.where(col_ids == token_at + tokens, rates, 0.0).astype(jnp.bfloat16)
+            gate_cols = dot(gates, all_ones).astype(jnp.bfloat16)
+            cums.append(dot(lower_ones, gate_cols))
+            betas.append(dot(writes, all_ones))
+
+        for i, at in enumerate(slabs):
+            pltpu.make_async_copy(recv.at[at], recv.at[at], recv_sem.at[first + i]).wait()
+
+        parts = []
+        for n in range(count):
+            queries = recv[slabs[n], :, 0:tokens, :].reshape(slab, width)
+            keys = recv[slabs[n], :, tokens : 2 * tokens, :].reshape(slab, width)
+            values = recv[slabs[n], :, 2 * tokens : 3 * tokens, :].reshape(slab, width)
+            cum, beta = cums[n], betas[n]
+            q32, k32 = queries.astype(jnp.float32), keys.astype(jnp.float32)
+            q_norm = 1.0 / jnp.sqrt(jnp.sum(q32 * q32, axis=1, keepdims=True) + 1e-06)
+            k_norm = 1.0 / jnp.sqrt(jnp.sum(k32 * k32, axis=1, keepdims=True) + 1e-06)
+            columns = jnp.where(col_ids == 0, cum, jnp.where(col_ids == 1, k_norm, beta))
+            rows = columns.T
+            cum_row, k_norm_row, beta_row = rows[0:1, :], rows[1:2, :], rows[2:3, :]
+            k_turned = k32.T.astype(jnp.bfloat16)
+            decay = jnp.where(inclusive, jnp.exp(jnp.where(inclusive, cum - cum_row, 0.0)), 0.0)
+            decay = decay * k_norm_row
+            key_key = dot(keys, k_turned)
+            query_key = dot(queries, k_turned)
+            lower = jnp.where(strict, (beta * k_norm) * decay * key_key, 0.0)
+            scores = q_norm * decay * query_key
+            parts.append((queries, keys, values, cum, k_norm, q_norm, cum_row, k_norm_row, beta_row,
+                          k_turned, lower, scores, q32))
+
+        small = 32
+        same = (row_ids // small) == (col_ids // small)
+        lowers = [part[10] for part in parts]
+        blocks = [jnp.where(same, lower, 0.0) for lower in lowers]
+        inverses = [eye - block for block in blocks]
+        powers = [mul(block, block) for block in blocks]
+        reach = 2
+        while reach < small:
+            last = reach * 2 >= small
+            for n in range(count):
+                right = tall(powers[n])
+                if last:
+                    inverses[n] = inverses[n] + fold(dot(wide(inverses[n]), right))
+                else:
+                    left = jnp.concatenate([wide(inverses[n]), wide(powers[n])], axis=0)
+                    both_products = fold(dot(left, right))
+                    inverses[n] = inverses[n] + both_products[:slab]
+                    powers[n] = both_products[slab:]
+            reach *= 2
+        size = small
+        while size < slab:
+            pair = ((row_ids // (2 * size)) == (col_ids // (2 * size))) & (
+                (row_ids // size) != (col_ids // size)
+            )
+            inner = [mul(jnp.where(pair, lowers[n], 0.0), inverses[n]) for n in range(count)]
+            inverses = [inverses[n] - mul(inverses[n], inner[n]) for n in range(count)]
+            size *= 2
+
+        for n in range(count):
+            (queries, keys, values, cum, k_norm, q_norm, cum_row, k_norm_row, beta_row,
+             k_turned, lower, scores, q32) = parts[n]
+            solve = inverses[n] * beta_row
+            write_vals = dot(wide(solve), jnp.concatenate([values, values], axis=0))
+            final = cum[slab - 1 : slab, :]
+            key_decay = jnp.exp(final - cum) * k_norm
+            key_solve = solve * (jnp.exp(cum_row) * k_norm_row)
+            write_keys = dot(wide(key_solve), jnp.concatenate([keys, keys], axis=0))
+            scaled = jnp.concatenate([wide(key_decay * write_keys), wide(key_decay * write_vals)], axis=1)
+            moved = dot(k_turned, scaled)
+            read = dot(wide(scores), tall(write_keys, write_vals))
+            project = (jnp.exp(cum) * q_norm) * q32 - fold(read[:, : 2 * width])
+            at = slabs[n]
+            step_maps[at, :slab, :] = wide(fold(moved[:, : 2 * width]))
+            step_maps[at, slab:, :] = wide(project)
+            step_terms[at, :slab, :] = fold(moved[:, 2 * width :])
+            step_terms[at, slab:, :] = fold(read[:, 2 * width :])
+            step_decay[at, :, :] = jnp.exp(final)
+
+    columns = pl.ds(pl.multiple_of(mine * width, width), width)
     state = None
     for n in range(ns):
-        erase, project, inject, direct, total_decay = maps[n]
         if n == 0:
-            output, state = direct, inject
+            state, output = step_terms[n, :slab, :], step_terms[n, slab:, :]
         else:
-            right = tall(state)
-            products = fold(dot(jnp.concatenate([wide(erase), wide(project)], axis=0), right))
-            output = direct + products[slab:]
-            state = total_decay * state + inject - products[:slab]
+            products = fold(dot(step_maps[n], tall(state)))
+            output = step_terms[n, slab:, :] + products[slab:]
+            state = step_decay[n] * state + step_terms[n, :slab, :] - products[:slab]
         out_buf[n * nh : (n + 1) * nh] = output.astype(jnp.bfloat16).reshape(nh, tokens, width)
         state_buf[n] = state
 
-    columns = pl.ds(pl.multiple_of(mine * width, width), width)
-    for i, (ps, ph) in enumerate(peers):
-        block = out_buf.at[ps * nh + ph]
-        target = out_ref.at[:, columns]
-        if i == 0:
-            pltpu.make_async_copy(block, target, recv_sem.at[2]).start()
-            pltpu.make_async_copy(state_buf.at[s], states_ref.at[0, s], recv_sem.at[3]).start()
-        else:
+        @pl.when(s == n)
+        def _():
+            pltpu.make_async_copy(state_buf.at[n], states_ref.at[0, s], back_sem.at[1]).start()
+
+        @pl.when(s != n)
+        def _():
             pltpu.make_async_remote_copy(
-                src_ref=block,
-                dst_ref=target,
-                send_sem=send_sem.at[2],
-                recv_sem=recv_sem.at[2],
-                device_id=(ps, ph),
+                src_ref=state_buf.at[n],
+                dst_ref=states_ref.at[0, s],
+                send_sem=send_sem.at[3],
+                recv_sem=back_sem.at[1],
+                device_id=(n, h),
                 device_id_type=MESH,
             ).start()
-        if i > 0 and i % nh == 0:
+
+        def give(ph):
             pltpu.make_async_remote_copy(
-                src_ref=state_buf.at[ps],
-                dst_ref=states_ref.at[0, s],
-                send_sem=send_sem.at[3],
-                recv_sem=recv_sem.at[3],
-                device_id=(ps, h),
+                src_ref=out_buf.at[n * nh + ph],
+                dst_ref=out_ref.at[:, columns],
+                send_sem=send_sem.at[2],
+                recv_sem=back_sem.at[0],
+                device_id=(n, ph),
                 device_id_type=MESH,
             ).start()
+
+        for dh in range(1, nh):
+            give(lax.rem(h + dh, nh))
+
+        @pl.when(s == n)
+        def _():
+            pltpu.make_async_copy(
+                out_buf.at[n * nh + h], out_ref.at[:, columns], back_sem.at[0]
+            ).start()
+
+        @pl.when(s != n)
+        def _():
+            give(h)
 
     others = pl.ds(0, ns * nh - 1)
     pltpu.make_async_copy(send.at[others], send.at[others], send_sem.at[0]).wait()
@@ -401,8 +420,8 @@
     pltpu.make_async_copy(out_buf.at[others], out_buf.at[others], send_sem.at[2]).wait()
     rest = state_buf.at[pl.ds(0, ns - 1)]
     pltpu.make_async_copy(rest, rest, send_sem.at[3]).wait()
-    pltpu.make_async_copy(out_ref, out_ref, recv_sem.at[2]).wait()
-    pltpu.make_async_copy(states_ref, states_ref, recv_sem.at[3]).wait()
+    pltpu.make_async_copy(out_ref, out_ref, back_sem.at[0]).wait()
+    pltpu.make_async_copy(states_ref, states_ref, back_sem.at[1]).wait()
 
 
 def fast_device(query_heads, key_heads, value_heads, gate_log, beta_rate):
@@ -411,15 +430,15 @@
     key_count = key_heads.shape[1]
     sizes = (ns, nh, tokens, heads, heads // key_count)
     bf16, f32 = jnp.bfloat16, jnp.float32
-    vmem = pl.BlockSpec(memory_space=pltpu.VMEM)
+    anywhere = pl.BlockSpec(memory_space=pl.ANY)
     return pl.pallas_call(
         functools.partial(fast_kernel, sizes),
         out_shape=(
             jax.ShapeDtypeStruct((tokens, heads * width), bf16),
             jax.ShapeDtypeStruct((1, ns, width, width), f32),
         ),
-        in_specs=[pl.BlockSpec(memory_space=pl.ANY)] * 5,
-        out_specs=(vmem, vmem),
+        in_specs=[anywhere] * 5,
+        out_specs=(anywhere, anywhere),
         scratch_shapes=[
             pltpu.VMEM((tokens, key_count, width), bf16),
             pltpu.VMEM((tokens, key_count, width), bf16),
@@ -435,12 +454,17 @@
             pltpu.VMEM((ns, nh, 1, width), f32),
             pltpu.VMEM((ns * nh, tokens, width), bf16),
             pltpu.VMEM((ns, width, width), f32),
+            pltpu.VMEM((ns, 2 * width, 2 * width), bf16),
+            pltpu.VMEM((ns, 2 * width, width), f32),
+            pltpu.VMEM((ns, 1, width), f32),
             pltpu.SemaphoreType.DMA((5,)),
             pltpu.SemaphoreType.DMA((4,)),
-            pltpu.SemaphoreType.DMA((4,)),
+            pltpu.SemaphoreType.DMA((ns,)),
+            pltpu.SemaphoreType.DMA((ns,)),
+            pltpu.SemaphoreType.DMA((2,)),
         ],
         compiler_params=pltpu.CompilerParams(
-            collective_id=0, has_side_effects=True, vmem_limit_bytes=32 * 1024 * 1024
+            collective_id=0, has_side_effects=True, vmem_limit_bytes=60 * 1024 * 1024
         ),
     )(query_heads, key_heads, value_heads, gate_log, beta_rate)
 

time: 34.9 us -> 29.9 us (0.86)
  local copies, waits for them, and re-layouts: 5.31 us -> 2.32 us
  Pallas kernels: 28.5 us -> 26.8 us
    unnamed x12 -> x4, local copies, waits for them, and re-layouts: 5.31 us -> 2.32 us
    pallas_call x1, Pallas kernels: 28.5 us -> 26.8 us  [fast_device(): pl.pallas_call(functools.partial(fast_kernel, sizes), out_shape=(jax.Shap...]
where the time goes in v2:
time: 29.9 us; the launch traced here: 29.8 us
  Pallas kernels  26.8 us (90%)
  local copies, waits for them, and re-layouts  2.32 us (8%)
  between operations  0.65 us (2%)
    pallas_call x1, Pallas kernels, fast_device(): pl.pallas_call(functools.partial(fast_kernel, sizes), out_shape=(jax.Shap...  26.8 us
    unnamed x4, local copies, waits for them, and re-layouts  2.32 us

profile of v2, /device:TPU:1, one launch (start us, length us, event | category | flops | bytes accessed | tf_op | source)
XLA Modules:
  0.0 29.8 jit_solution(4563273583065910411)
XLA Ops:
  0.6 26.8 %shard_map.68 = (bf16[16,4096]{1,0:T(8,128)(2,1)}, f32[1,4,128,128]{3,2,1,0:T(8,128)}) custom-call(bf16[16,16,128]{2,1,0:T(8,128)(2,1)} %q_hbm.1, bf16[16,16,128]{2,1,0:T(8,128)(2,1)} %k_hbm.1, bf16[16,32,128]{2,1,0:T(8,128)(2,1)} %v_hbm.1, bf16[16,32]{1,0:T(8,128)(2,1)} %g_hbm.1, bf16[16,32]{1,0:T(8,128)(2,1)} %b_hbm.1), custom_call_target="tpu_custom_call" | custom-call | tf_op jit(solution)/shard_map/pallas_call | solution.py:434
  27.5 0.0 copy-start
  27.5 1.6 %copy.9 = bf16[16,4096]{1,0:T(8,128)(2,1)} copy(bf16[16,4096]{1,0:T(8,128)(2,1)} %get-tuple-element.4) | data formatting | bytes 262144
  29.1 0.0 copy-done
  29.1 0.7 %copy.10 = f32[1,4,128,128]{3,2,1,0:T(8,128)} copy(f32[1,4,128,128]{3,2,1,0:T(8,128)S(1)} %copy-done) | data formatting | bytes 524288
Async XLA Ops:
  27.5 1.6 %copy-start = (f32[1,4,128,128]{3,2,1,0:T(8,128)S(1)}, f32[1,4,128,128]{3,2,1,0:T(8,128)}, u32[]{:S(2)}) copy-start(f32[1,4,128,128]{3,2,1,0:T(8,128)} %get-tuple-element.5) | copy-start | bytes 786436

commit v3 on v2

--- a/solution.py
+++ b/solution.py
@@ -186,6 +186,7 @@
     send,
     gb_send,
     recv,
+    swapped,
     gb_recv,
     out_buf,
     state_buf,
@@ -197,9 +198,9 @@
     recv_sem,
     gb_sem,
     back_sem,
+    swap_sem,
 ):
-    ns, nh, tokens, heads, grouping = sizes
-    key_heads = heads // grouping
+    ns, nh, tokens, heads, key_heads = sizes
     slab = nh * tokens
     width = 128
     s = lax.axis_index("seq")
@@ -216,9 +217,18 @@
         load.start()
 
     peers = []
-    for ds in range(ns):
+    seq_peers = [s]
+    for ds in range(1, ns):
+        other, bit = s, 1
+        while bit <= ds:
+            if ds & bit:
+                other = other + bit - 2 * bit * lax.rem(s // bit, 2)
+            bit *= 2
+        seq_peers.append(other)
+    for ps in seq_peers:
         for dh in range(nh):
-            peers.append((lax.rem(s + ds, ns), lax.rem(h + dh, nh)))
+            peers.append((ps, lax.rem(h + dh, nh)))
+    even = lax.rem(s, 2) == 0
 
     barrier = pltpu.get_barrier_semaphore()
     for ps, ph in peers[1:]:
@@ -232,12 +242,11 @@
     for j in range(key_heads):
         queries = q_wide[pl.ds(j, tokens, stride=key_heads), :].astype(jnp.bfloat16)
         keys = k_wide[pl.ds(j, tokens, stride=key_heads), :].astype(jnp.bfloat16)
-        for g in range(grouping):
-            send[j * grouping + g, 0:tokens, :] = queries
-            send[j * grouping + g, tokens : 2 * tokens, :] = keys
+        send[2 * j, 0:tokens, :] = queries
+        send[2 * j + 1, 0:tokens, :] = keys
     for j in range(heads):
         values = v_wide[pl.ds(j, tokens, stride=heads), :].astype(jnp.bfloat16)
-        send[j, 2 * tokens : 3 * tokens, :] = values
+        send[j, tokens : 2 * tokens, :] = values
     both = jnp.concatenate([g_in[...], b_in[...]], axis=0).astype(jnp.float32)
     place_row = lax.broadcasted_iota(jnp.int32, (2 * tokens, width), 0)
     place_col = lax.broadcasted_iota(jnp.int32, (2 * tokens, width), 1)
@@ -278,7 +287,7 @@
     ).astype(jnp.bfloat16)
 
     for first in range(0, ns, 2):
-        slabs = [lax.rem(s + ns - first - i, ns) for i in range(min(2, ns - first))]
+        slabs = seq_peers[first : first + 2]
         count = len(slabs)
         for i, at in enumerate(slabs):
             pltpu.make_async_copy(gb_recv.at[at], gb_recv.at[at], gb_sem.at[first + i]).wait()
@@ -293,12 +302,23 @@
 
         for i, at in enumerate(slabs):
             pltpu.make_async_copy(recv.at[at], recv.at[at], recv_sem.at[first + i]).wait()
+            pltpu.make_async_remote_copy(
+                src_ref=recv.at[at, :, 0:tokens, :],
+                dst_ref=swapped.at[at],
+                send_sem=send_sem.at[4],
+                recv_sem=swap_sem.at[first // 2],
+                device_id=(seq_peers[1], h),
+                device_id_type=MESH,
+            ).start()
+        two = swapped.at[pl.ds(0, count)]
+        pltpu.make_async_copy(two, two, swap_sem.at[first // 2]).wait()
 
         parts = []
         for n in range(count):
-            queries = recv[slabs[n], :, 0:tokens, :].reshape(slab, width)
-            keys = recv[slabs[n], :, tokens : 2 * tokens, :].reshape(slab, width)
-            values = recv[slabs[n], :, 2 * tokens : 3 * tokens, :].reshape(slab, width)
+            own = recv[slabs[n], :, 0:tokens, :].reshape(slab, width)
+            other = swapped[slabs[n]].reshape(slab, width)
+            queries, keys = jnp.where(even, own, other), jnp.where(even, other, own)
+            values = recv[slabs[n], :, tokens : 2 * tokens, :].reshape(slab, width)
             cum, beta = cums[n], betas[n]
             q32, k32 = queries.astype(jnp.float32), keys.astype(jnp.float32)
             q_norm = 1.0 / jnp.sqrt(jnp.sum(q32 * q32, axis=1, keepdims=True) + 1e-06)
@@ -418,6 +438,7 @@
     pltpu.make_async_copy(send.at[others], send.at[others], send_sem.at[0]).wait()
     pltpu.make_async_copy(gb_send.at[others], gb_send.at[others], send_sem.at[1]).wait()
     pltpu.make_async_copy(out_buf.at[others], out_buf.at[others], send_sem.at[2]).wait()
+    pltpu.make_async_copy(swapped, swapped, send_sem.at[4]).wait()
     rest = state_buf.at[pl.ds(0, ns - 1)]
     pltpu.make_async_copy(rest, rest, send_sem.at[3]).wait()
     pltpu.make_async_copy(out_ref, out_ref, back_sem.at[0]).wait()
@@ -428,7 +449,7 @@
     ns, nh = lax.axis_size("seq"), lax.axis_size("head")
     tokens, heads, width = value_heads.shape
     key_count = key_heads.shape[1]
-    sizes = (ns, nh, tokens, heads, heads // key_count)
+    sizes = (ns, nh, tokens, heads, key_count)
     bf16, f32 = jnp.bfloat16, jnp.float32
     anywhere = pl.BlockSpec(memory_space=pl.ANY)
     return pl.pallas_call(
@@ -448,9 +469,10 @@
             pltpu.VMEM((tokens * key_count, width), f32),
             pltpu.VMEM((tokens * key_count, width), f32),
             pltpu.VMEM((tokens * heads, width), f32),
-            pltpu.VMEM((heads, 3 * tokens, width), bf16),
+            pltpu.VMEM((heads, 2 * tokens, width), bf16),
             pltpu.VMEM((heads, 1, width), f32),
-            pltpu.VMEM((ns, nh, 3 * tokens, width), bf16),
+            pltpu.VMEM((ns, nh, 2 * tokens, width), bf16),
+            pltpu.VMEM((ns, nh, tokens, width), bf16),
             pltpu.VMEM((ns, nh, 1, width), f32),
             pltpu.VMEM((ns * nh, tokens, width), bf16),
             pltpu.VMEM((ns, width, width), f32),
@@ -458,10 +480,11 @@
             pltpu.VMEM((ns, 2 * width, width), f32),
             pltpu.VMEM((ns, 1, width), f32),
             pltpu.SemaphoreType.DMA((5,)),
-            pltpu.SemaphoreType.DMA((4,)),
+            pltpu.SemaphoreType.DMA((5,)),
             pltpu.SemaphoreType.DMA((ns,)),
             pltpu.SemaphoreType.DMA((ns,)),
             pltpu.SemaphoreType.DMA((2,)),
+            pltpu.SemaphoreType.DMA((ns // 2,)),
         ],
         compiler_params=pltpu.CompilerParams(
             collective_id=0, has_side_effects=True, vmem_limit_bytes=60 * 1024 * 1024
@@ -474,6 +497,7 @@
     tokens, heads, width = value_heads.shape
     fits = ns * nh == heads and tokens == 16 and nh * tokens == 128
     fits = fits and width == 128 and key_heads.shape[2] == 128
+    fits = fits and heads == 2 * key_heads.shape[1] and ns in (2, 4, 8)
     run = fast_device if fits else per_device
     return run(query_heads, key_heads, value_heads, gate_log, beta_rate)
 

time: 29.9 us -> 29.9 us (level)
  no operation moved by 1% of the time
where the time goes in v3:
time: 29.9 us; the launch traced here: 29.8 us
  Pallas kernels  26.8 us (90%)
  local copies, waits for them, and re-layouts  2.32 us (8%)
  between operations  0.65 us (2%)
    pallas_call x1, Pallas kernels, fast_device(): pl.pallas_call(functools.partial(fast_kernel, sizes), out_shape=(jax.Shap...  26.8 us
    unnamed x4, local copies, waits for them, and re-layouts  2.32 us

profile of v3, /device:TPU:1, one launch (start us, length us, event | category | flops | bytes accessed | tf_op | source)
XLA Modules:
  0.0 29.8 jit_solution(18318869867887806789)
XLA Ops:
  0.6 26.8 %shard_map.68 = (bf16[16,4096]{1,0:T(8,128)(2,1)}, f32[1,4,128,128]{3,2,1,0:T(8,128)}) custom-call(bf16[16,16,128]{2,1,0:T(8,128)(2,1)} %q_hbm.1, bf16[16,16,128]{2,1,0:T(8,128)(2,1)} %k_hbm.1, bf16[16,32,128]{2,1,0:T(8,128)(2,1)} %v_hbm.1, bf16[16,32]{1,0:T(8,128)(2,1)} %g_hbm.1, bf16[16,32]{1,0:T(8,128)(2,1)} %b_hbm.1), custom_call_target="tpu_custom_call" | custom-call | tf_op jit(solution)/shard_map/pallas_call | solution.py:455
  27.4 0.0 copy-start
  27.5 1.6 %copy.9 = bf16[16,4096]{1,0:T(8,128)(2,1)} copy(bf16[16,4096]{1,0:T(8,128)(2,1)} %get-tuple-element.4) | data formatting | bytes 262144
  29.1 0.0 copy-done
  29.1 0.7 %copy.10 = f32[1,4,128,128]{3,2,1,0:T(8,128)} copy(f32[1,4,128,128]{3,2,1,0:T(8,128)S(1)} %copy-done) | data formatting | bytes 524288
Async XLA Ops:
  27.4 1.6 %copy-start = (f32[1,4,128,128]{3,2,1,0:T(8,128)S(1)}, f32[1,4,128,128]{3,2,1,0:T(8,128)}, u32[]{:S(2)}) copy-start(f32[1,4,128,128]{3,2,1,0:T(8,128)} %get-tuple-element.5) | copy-start | bytes 786436

commit v4 on v3

--- a/solution.py
+++ b/solution.py
@@ -184,10 +184,9 @@
     k_wide,
     v_wide,
     send,
-    gb_send,
     recv,
     swapped,
-    gb_recv,
+    gb_all,
     out_buf,
     state_buf,
     step_maps,
@@ -247,31 +246,44 @@
     for j in range(heads):
         values = v_wide[pl.ds(j, tokens, stride=heads), :].astype(jnp.bfloat16)
         send[j, tokens : 2 * tokens, :] = values
-    both = jnp.concatenate([g_in[...], b_in[...]], axis=0).astype(jnp.float32)
-    place_row = lax.broadcasted_iota(jnp.int32, (2 * tokens, width), 0)
-    place_col = lax.broadcasted_iota(jnp.int32, (2 * tokens, width), 1)
-    place = (place_row == place_col).astype(jnp.bfloat16)
-    turned = dot(both.T.astype(jnp.bfloat16), place)
-    for j in range(heads):
-        gb_send[j, :, :] = turned[j : j + 1, :]
+    pad = jnp.zeros((tokens, width - 2 * heads), jnp.bfloat16)
+    gb_all[s, h] = jnp.concatenate([g_in[...], b_in[...], pad], axis=1)
 
     pl.semaphore_wait(barrier, ns * nh - 1)
 
+    for dh in range(1, nh):
+        pltpu.make_async_remote_copy(
+            src_ref=gb_all.at[s, h],
+            dst_ref=gb_all.at[s, h],
+            send_sem=send_sem.at[1],
+            recv_sem=gb_sem.at[0],
+            device_id=(s, lax.rem(h + dh, nh)),
+            device_id_type=MESH,
+        ).start()
     for i, (ps, ph) in enumerate(peers):
         j = ph * ns + ps
         if i == 0:
             pltpu.make_async_copy(send.at[j], recv.at[s, h], recv_sem.at[0]).start()
-            pltpu.make_async_copy(gb_send.at[j], gb_recv.at[s, h], gb_sem.at[0]).start()
         else:
-            for source, target, n, sem in ((gb_send, gb_recv, 1, gb_sem), (send, recv, 0, recv_sem)):
-                pltpu.make_async_remote_copy(
-                    src_ref=source.at[j],
-                    dst_ref=target.at[s, h],
-                    send_sem=send_sem.at[n],
-                    recv_sem=sem.at[i // nh],
-                    device_id=(ps, ph),
-                    device_id_type=MESH,
-                ).start()
+            pltpu.make_async_remote_copy(
+                src_ref=send.at[j],
+                dst_ref=recv.at[s, h],
+                send_sem=send_sem.at[0],
+                recv_sem=recv_sem.at[i // nh],
+                device_id=(ps, ph),
+                device_id_type=MESH,
+            ).start()
+    head_others = gb_all.at[0, pl.ds(0, nh - 1)]
+    pltpu.make_async_copy(head_others, head_others, gb_sem.at[0]).wait()
+    for ps in seq_peers[1:]:
+        pltpu.make_async_remote_copy(
+            src_ref=gb_all.at[s],
+            dst_ref=gb_all.at[s],
+            send_sem=send_sem.at[5],
+            recv_sem=gb_sem.at[1],
+            device_id=(ps, h),
+            device_id_type=MESH,
+        ).start()
 
     row_ids = lax.broadcasted_iota(jnp.int32, (slab, slab), 0)
     col_ids = lax.broadcasted_iota(jnp.int32, (slab, slab), 1)
@@ -279,27 +291,22 @@
     inclusive = row_ids >= col_ids
     eye = (row_ids == col_ids).astype(jnp.float32)
     lower_ones = inclusive.astype(jnp.bfloat16)
-    all_ones = jnp.ones((slab, slab), jnp.bfloat16)
-    token_at = row_ids % tokens
-    expand = (
-        lax.broadcasted_iota(jnp.int32, (slab, nh), 0) // tokens
-        == lax.broadcasted_iota(jnp.int32, (slab, nh), 1)
-    ).astype(jnp.bfloat16)
+    pick_row = lax.broadcasted_iota(jnp.int32, (width, 2 * slab), 0)
+    pick_col = lax.broadcasted_iota(jnp.int32, (width, 2 * slab), 1)
+    pick = (pick_row == mine + heads * (pick_col // slab)).astype(jnp.bfloat16)
+
+    seq_others = gb_all.at[pl.ds(0, ns - 1)]
+    pltpu.make_async_copy(seq_others, seq_others, gb_sem.at[1]).wait()
+    all_cums, all_betas = [], []
+    for at in seq_peers:
+        picked = dot(gb_all[at].reshape(slab, width), pick)
+        all_cums.append(dot(lower_ones, picked[:, :slab].astype(jnp.bfloat16)))
+        all_betas.append(picked[:, slab:])
 
     for first in range(0, ns, 2):
         slabs = seq_peers[first : first + 2]
         count = len(slabs)
-        for i, at in enumerate(slabs):
-            pltpu.make_async_copy(gb_recv.at[at], gb_recv.at[at], gb_sem.at[first + i]).wait()
-        cums, betas = [], []
-        for at in slabs:
-            rates = dot(expand, gb_recv[at, :, 0, :].astype(jnp.bfloat16))
-            gates = jnp.where(col_ids == token_at, rates, 0.0).astype(jnp.bfloat16)
-            writes = jnp.where(col_ids == token_at + tokens, rates, 0.0).astype(jnp.bfloat16)
-            gate_cols = dot(gates, all_ones).astype(jnp.bfloat16)
-            cums.append(dot(lower_ones, gate_cols))
-            betas.append(dot(writes, all_ones))
-
+        cums, betas = all_cums[first : first + 2], all_betas[first : first + 2]
         for i, at in enumerate(slabs):
             pltpu.make_async_copy(recv.at[at], recv.at[at], recv_sem.at[first + i]).wait()
             pltpu.make_async_remote_copy(
@@ -436,13 +443,25 @@
 
     others = pl.ds(0, ns * nh - 1)
     pltpu.make_async_copy(send.at[others], send.at[others], send_sem.at[0]).wait()
-    pltpu.make_async_copy(gb_send.at[others], gb_send.at[others], send_sem.at[1]).wait()
+    pltpu.make_async_copy(head_others, head_others, send_sem.at[1]).wait()
+    pltpu.make_async_copy(seq_others, seq_others, send_sem.at[5]).wait()
     pltpu.make_async_copy(out_buf.at[others], out_buf.at[others], send_sem.at[2]).wait()
     pltpu.make_async_copy(swapped, swapped, send_sem.at[4]).wait()
     rest = state_buf.at[pl.ds(0, ns - 1)]
     pltpu.make_async_copy(rest, rest, send_sem.at[3]).wait()
     pltpu.make_async_copy(out_ref, out_ref, back_sem.at[0]).wait()
     pltpu.make_async_copy(states_ref, states_ref, back_sem.at[1]).wait()
+
+
+def hand_over(rows_in, states_in, rows_out, states_out, sems):
+    copies = [
+        pltpu.make_async_copy(rows_in, rows_out, sems.at[0]),
+        pltpu.make_async_copy(states_in, states_out, sems.at[1]),
+    ]
+    for copy in copies:
+        copy.start()
+    for copy in copies:
+        copy.wait()
 
 
 def fast_device(query_heads, key_heads, value_heads, gate_log, beta_rate):
@@ -452,7 +471,7 @@
     sizes = (ns, nh, tokens, heads, key_count)
     bf16, f32 = jnp.bfloat16, jnp.float32
     anywhere = pl.BlockSpec(memory_space=pl.ANY)
-    return pl.pallas_call(
+    rows, states = pl.pallas_call(
         functools.partial(fast_kernel, sizes),
         out_shape=(
             jax.ShapeDtypeStruct((tokens, heads * width), bf16),
@@ -470,19 +489,18 @@
             pltpu.VMEM((tokens * key_count, width), f32),
             pltpu.VMEM((tokens * heads, width), f32),
             pltpu.VMEM((heads, 2 * tokens, width), bf16),
-            pltpu.VMEM((heads, 1, width), f32),
             pltpu.VMEM((ns, nh, 2 * tokens, width), bf16),
             pltpu.VMEM((ns, nh, tokens, width), bf16),
-            pltpu.VMEM((ns, nh, 1, width), f32),
+            pltpu.VMEM((ns, nh, tokens, width), bf16),
             pltpu.VMEM((ns * nh, tokens, width), bf16),
             pltpu.VMEM((ns, width, width), f32),
             pltpu.VMEM((ns, 2 * width, 2 * width), bf16),
             pltpu.VMEM((ns, 2 * width, width), f32),
             pltpu.VMEM((ns, 1, width), f32),
             pltpu.SemaphoreType.DMA((5,)),
-            pltpu.SemaphoreType.DMA((5,)),
+            pltpu.SemaphoreType.DMA((6,)),
             pltpu.SemaphoreType.DMA((ns,)),
-            pltpu.SemaphoreType.DMA((ns,)),
+            pltpu.SemaphoreType.DMA((2,)),
             pltpu.SemaphoreType.DMA((2,)),
             pltpu.SemaphoreType.DMA((ns // 2,)),
         ],
@@ -490,6 +508,17 @@
             collective_id=0, has_side_effects=True, vmem_limit_bytes=60 * 1024 * 1024
         ),
     )(query_heads, key_heads, value_heads, gate_log, beta_rate)
+    return pl.pallas_call(
+        hand_over,
+        out_shape=(
+            jax.ShapeDtypeStruct(rows.shape, bf16),
+            jax.ShapeDtypeStruct(states.shape, f32),
+        ),
+        in_specs=[anywhere] * 2,
+        out_specs=(anywhere, anywhere),
+        scratch_shapes=[pltpu.SemaphoreType.DMA((2,))],
+        compiler_params=pltpu.CompilerParams(vmem_limit_bytes=60 * 1024 * 1024),
+    )(rows, states)
 
 
 def choose_device(query_heads, key_heads, value_heads, gate_log, beta_rate):
@@ -497,7 +526,7 @@
     tokens, heads, width = value_heads.shape
     fits = ns * nh == heads and tokens == 16 and nh * tokens == 128
     fits = fits and width == 128 and key_heads.shape[2] == 128
-    fits = fits and heads == 2 * key_heads.shape[1] and ns in (2, 4, 8)
+    fits = fits and heads == 2 * key_heads.shape[1] and ns in (2, 4, 8) and 2 * heads < width
     run = fast_device if fits else per_device
     return run(query_heads, key_heads, value_heads, gate_log, beta_rate)
 

time: 29.9 us -> 41.9 us (1.40)
  Pallas kernels: 26.8 us -> 41.1 us
  local copies, waits for them, and re-layouts: 2.32 us -> 0 us
    pallas_call x0 -> x1, Pallas kernels: none -> 13 us  [fast_device(): pl.pallas_call(hand_over, out_shape=(jax.ShapeDtypeStruct(rows.shape, bf1...]
    unnamed x4 -> x0, local copies, waits for them, and re-layouts: 2.32 us -> none
    pallas_call x1, Pallas kernels: 26.8 us -> 28.1 us  [fast_device(): pl.pallas_call(functools.partial(fast_kernel, sizes), out_shape=(jax.Shap...]
where the time goes in v4:
time: 41.9 us; the launch traced here: 41.8 us
  Pallas kernels  41.1 us (98%)
  between operations  0.64 us (2%)
    pallas_call x1, Pallas kernels, fast_device(): pl.pallas_call(functools.partial(fast_kernel, sizes), out_shape=(jax.Shap...  28.1 us
    pallas_call x1, Pallas kernels, fast_device(): pl.pallas_call(hand_over, out_shape=(jax.ShapeDtypeStruct(rows.shape, bf1...  13 us

profile of v4, /device:TPU:1, one launch (start us, length us, event | category | flops | bytes accessed | tf_op | source)
XLA Modules:
  0.0 41.8 jit_solution(335938844776307871)
XLA Ops:
  0.6 28.1 %shard_map.68 = (bf16[16,4096]{1,0:T(8,128)(2,1)}, f32[1,4,128,128]{3,2,1,0:T(8,128)}) custom-call(bf16[16,16,128]{2,1,0:T(8,128)(2,1)} %q_hbm.1, bf16[16,16,128]{2,1,0:T(8,128)(2,1)} %k_hbm.1, bf16[16,32,128]{2,1,0:T(8,128)(2,1)} %v_hbm.1, bf16[16,32]{1,0:T(8,128)(2,1)} %g_hbm.1, bf16[16,32]{1,0:T(8,128)(2,1)} %b_hbm.1), custom_call_target="tpu_custom_call" | custom-call | tf_op jit(solution)/shard_map/pallas_call | solution.py:474
  28.7 13.0 %shard_map.69 = (bf16[16,4096]{1,0:T(8,128)(2,1)}, f32[1,4,128,128]{3,2,1,0:T(8,128)}) custom-call(bf16[16,4096]{1,0:T(8,128)(2,1)} %get-tuple-element.4.rows_in, f32[1,4,128,128]{3,2,1,0:T(8,128)} %get-tuple-element.5.states_in), custom_call_target="tpu_custom_call" | custom-call | tf_op jit(solution)/shard_map/pallas_call | solution.py:511

commit v5 on v3

--- a/solution.py
+++ b/solution.py
@@ -184,10 +184,8 @@
     k_wide,
     v_wide,
     send,
-    gb_send,
     recv,
     swapped,
-    gb_recv,
     out_buf,
     state_buf,
     step_maps,
@@ -196,7 +194,6 @@
     load_sem,
     send_sem,
     recv_sem,
-    gb_sem,
     back_sem,
     swap_sem,
 ):
@@ -247,13 +244,10 @@
     for j in range(heads):
         values = v_wide[pl.ds(j, tokens, stride=heads), :].astype(jnp.bfloat16)
         send[j, tokens : 2 * tokens, :] = values
-    both = jnp.concatenate([g_in[...], b_in[...]], axis=0).astype(jnp.float32)
-    place_row = lax.broadcasted_iota(jnp.int32, (2 * tokens, width), 0)
-    place_col = lax.broadcasted_iota(jnp.int32, (2 * tokens, width), 1)
-    place = (place_row == place_col).astype(jnp.bfloat16)
-    turned = dot(both.T.astype(jnp.bfloat16), place)
+    pad = jnp.zeros((tokens, width - 2 * heads), jnp.bfloat16)
+    rates = jnp.concatenate([g_in[...], b_in[...], pad], axis=1)
     for j in range(heads):
-        gb_send[j, :, :] = turned[j : j + 1, :]
+        send[j, 2 * tokens : 3 * tokens, :] = rates
 
     pl.semaphore_wait(barrier, ns * nh - 1)
 
@@ -261,45 +255,28 @@
         j = ph * ns + ps
         if i == 0:
             pltpu.make_async_copy(send.at[j], recv.at[s, h], recv_sem.at[0]).start()
-            pltpu.make_async_copy(gb_send.at[j], gb_recv.at[s, h], gb_sem.at[0]).start()
         else:
-            for source, target, n, sem in ((gb_send, gb_recv, 1, gb_sem), (send, recv, 0, recv_sem)):
-                pltpu.make_async_remote_copy(
-                    src_ref=source.at[j],
-                    dst_ref=target.at[s, h],
-                    send_sem=send_sem.at[n],
-                    recv_sem=sem.at[i // nh],
-                    device_id=(ps, ph),
-                    device_id_type=MESH,
-                ).start()
-
+            pltpu.make_async_remote_copy(
+                src_ref=send.at[j],
+                dst_ref=recv.at[s, h],
+                send_sem=send_sem.at[0],
+                recv_sem=recv_sem.at[i // nh],
+                device_id=(ps, ph),
+                device_id_type=MESH,
+            ).start()
     row_ids = lax.broadcasted_iota(jnp.int32, (slab, slab), 0)
     col_ids = lax.broadcasted_iota(jnp.int32, (slab, slab), 1)
     strict = row_ids > col_ids
     inclusive = row_ids >= col_ids
     eye = (row_ids == col_ids).astype(jnp.float32)
     lower_ones = inclusive.astype(jnp.bfloat16)
-    all_ones = jnp.ones((slab, slab), jnp.bfloat16)
-    token_at = row_ids % tokens
-    expand = (
-        lax.broadcasted_iota(jnp.int32, (slab, nh), 0) // tokens
-        == lax.broadcasted_iota(jnp.int32, (slab, nh), 1)
-    ).astype(jnp.bfloat16)
+    pick_row = lax.broadcasted_iota(jnp.int32, (width, 2 * slab), 0)
+    pick_col = lax.broadcasted_iota(jnp.int32, (width, 2 * slab), 1)
+    pick = (pick_row == mine + heads * (pick_col // slab)).astype(jnp.bfloat16)
 
     for first in range(0, ns, 2):
         slabs = seq_peers[first : first + 2]
         count = len(slabs)
-        for i, at in enumerate(slabs):
-            pltpu.make_async_copy(gb_recv.at[at], gb_recv.at[at], gb_sem.at[first + i]).wait()
-        cums, betas = [], []
-        for at in slabs:
-            rates = dot(expand, gb_recv[at, :, 0, :].astype(jnp.bfloat16))
-            gates = jnp.where(col_ids == token_at, rates, 0.0).astype(jnp.bfloat16)
-            writes = jnp.where(col_ids == token_at + tokens, rates, 0.0).astype(jnp.bfloat16)
-            gate_cols = dot(gates, all_ones).astype(jnp.bfloat16)
-            cums.append(dot(lower_ones, gate_cols))
-            betas.append(dot(writes, all_ones))
-
         for i, at in enumerate(slabs):
             pltpu.make_async_copy(recv.at[at], recv.at[at], recv_sem.at[first + i]).wait()
             pltpu.make_async_remote_copy(
@@ -319,7 +296,9 @@
             other = swapped[slabs[n]].reshape(slab, width)
             queries, keys = jnp.where(even, own, other), jnp.where(even, other, own)
             values = recv[slabs[n], :, tokens : 2 * tokens, :].reshape(slab, width)
-            cum, beta = cums[n], betas[n]
+            rates = recv[slabs[n], :, 2 * tokens : 3 * tokens, :].reshape(slab, width)
+            picked = dot(rates, pick)
+            cum, beta = dot(lower_ones, picked[:, :slab].astype(jnp.bfloat16)), picked[:, slab:]
             q32, k32 = queries.astype(jnp.float32), keys.astype(jnp.float32)
             q_norm = 1.0 / jnp.sqrt(jnp.sum(q32 * q32, axis=1, keepdims=True) + 1e-06)
             k_norm = 1.0 / jnp.sqrt(jnp.sum(k32 * k32, axis=1, keepdims=True) + 1e-06)
@@ -436,7 +415,6 @@
 
     others = pl.ds(0, ns * nh - 1)
     pltpu.make_async_copy(send.at[others], send.at[others], send_sem.at[0]).wait()
-    pltpu.make_async_copy(gb_send.at[others], gb_send.at[others], send_sem.at[1]).wait()
     pltpu.make_async_copy(out_buf.at[others], out_buf.at[others], send_sem.at[2]).wait()
     pltpu.make_async_copy(swapped, swapped, send_sem.at[4]).wait()
     rest = state_buf.at[pl.ds(0, ns - 1)]
@@ -455,11 +433,11 @@
     return pl.pallas_call(
         functools.partial(fast_kernel, sizes),
         out_shape=(
-            jax.ShapeDtypeStruct((tokens, heads * width), bf16),
-            jax.ShapeDtypeStruct((1, ns, width, width), f32),
+            pltpu.VMEM((tokens, heads * width), bf16),
+            pltpu.VMEM((1, ns, width, width), f32),
         ),
         in_specs=[anywhere] * 5,
-        out_specs=(anywhere, anywhere),
+        out_specs=(pl.BlockSpec(memory_space=pltpu.VMEM),) * 2,
         scratch_shapes=[
             pltpu.VMEM((tokens, key_count, width), bf16),
             pltpu.VMEM((tokens, key_count, width), bf16),
@@ -469,11 +447,9 @@
             pltpu.VMEM((tokens * key_count, width), f32),
             pltpu.VMEM((tokens * key_count, width), f32),
             pltpu.VMEM((tokens * heads, width), f32),
-            pltpu.VMEM((heads, 2 * tokens, width), bf16),
-            pltpu.VMEM((heads, 1, width), f32),
-            pltpu.VMEM((ns, nh, 2 * tokens, width), bf16),
+            pltpu.VMEM((heads, 3 * tokens, width), bf16),
+            pltpu.VMEM((ns, nh, 3 * tokens, width), bf16),
             pltpu.VMEM((ns, nh, tokens, width), bf16),
-            pltpu.VMEM((ns, nh, 1, width), f32),
             pltpu.VMEM((ns * nh, tokens, width), bf16),
             pltpu.VMEM((ns, width, width), f32),
             pltpu.VMEM((ns, 2 * width, 2 * width), bf16),
@@ -482,7 +458,6 @@
             pltpu.SemaphoreType.DMA((5,)),
             pltpu.SemaphoreType.DMA((5,)),
             pltpu.SemaphoreType.DMA((ns,)),
-            pltpu.SemaphoreType.DMA((ns,)),
             pltpu.SemaphoreType.DMA((2,)),
             pltpu.SemaphoreType.DMA((ns // 2,)),
         ],
@@ -497,7 +472,7 @@
     tokens, heads, width = value_heads.shape
     fits = ns * nh == heads and tokens == 16 and nh * tokens == 128
     fits = fits and width == 128 and key_heads.shape[2] == 128
-    fits = fits and heads == 2 * key_heads.shape[1] and ns in (2, 4, 8)
+    fits = fits and heads == 2 * key_heads.shape[1] and ns in (2, 4, 8) and 2 * heads < width
     run = fast_device if fits else per_device
     return run(query_heads, key_heads, value_heads, gate_log, beta_rate)
 

time: 29.9 us -> 30 us (level)
  Pallas kernels: 26.8 us -> 27.9 us
  local copies, waits for them, and re-layouts: 2.32 us -> 1.36 us
    pallas_call x1, Pallas kernels: 26.8 us -> 27.9 us  [fast_device(): pl.pallas_call(functools.partial(fast_kernel, sizes), out_shape=(pltpu.VM...]
    unnamed x4 -> x2, local copies, waits for them, and re-layouts: 2.32 us -> 1.36 us
where the time goes in v5:
time: 30 us; the launch traced here: 29.9 us
  Pallas kernels  27.9 us (93%)
  local copies, waits for them, and re-layouts  1.36 us (5%)
  between operations  0.64 us (2%)
    pallas_call x1, Pallas kernels, fast_device(): pl.pallas_call(functools.partial(fast_kernel, sizes), out_shape=(pltpu.VM...  27.9 us
    unnamed x2, local copies, waits for them, and re-layouts  1.36 us

profile of v5, /device:TPU:1, one launch (start us, length us, event | category | flops | bytes accessed | tf_op | source)
XLA Modules:
  0.0 29.9 jit_solution(13218609641313100673)
XLA Ops:
  0.6 27.9 %shard_map.68 = (bf16[16,4096]{1,0:T(8,128)(2,1)S(1)}, f32[1,4,128,128]{3,2,1,0:T(8,128)S(1)}) custom-call(bf16[16,16,128]{2,1,0:T(8,128)(2,1)} %q_hbm.1, bf16[16,16,128]{2,1,0:T(8,128)(2,1)} %k_hbm.1, bf16[16,32,128]{2,1,0:T(8,128)(2,1)} %v_hbm.1, bf16[16,32]{1,0:T(8,128)(2,1)} %g_hbm.1, bf16[16,32]{1,0:T(8,128)(2,1)} %b_hbm.1), custom_call_target="tpu_custom_call" | custom-call | tf_op jit(solution)/shard_map/pallas_call | solution.py:433
  28.5 0.7 %copy.9 = bf16[16,4096]{1,0:T(8,128)(2,1)} copy(bf16[16,4096]{1,0:T(8,128)(2,1)S(1)} %get-tuple-element.2) | data formatting | bytes 262144
  29.2 0.7 %copy.10 = f32[1,4,128,128]{3,2,1,0:T(8,128)} copy(f32[1,4,128,128]{3,2,1,0:T(8,128)S(1)} %get-tuple-element.3) | data formatting | bytes 524288

commit v6 on v3

--- a/solution.py
+++ b/solution.py
@@ -445,6 +445,17 @@
     pltpu.make_async_copy(states_ref, states_ref, back_sem.at[1]).wait()
 
 
+def hand_over(rows_in, states_in, rows_out, states_out, sems):
+    copies = [
+        pltpu.make_async_copy(rows_in, rows_out, sems.at[0]),
+        pltpu.make_async_copy(states_in, states_out, sems.at[1]),
+    ]
+    for copy in copies:
+        copy.start()
+    for copy in copies:
+        copy.wait()
+
+
 def fast_device(query_heads, key_heads, value_heads, gate_log, beta_rate):
     ns, nh = lax.axis_size("seq"), lax.axis_size("head")
     tokens, heads, width = value_heads.shape
@@ -452,14 +463,15 @@
     sizes = (ns, nh, tokens, heads, key_count)
     bf16, f32 = jnp.bfloat16, jnp.float32
     anywhere = pl.BlockSpec(memory_space=pl.ANY)
-    return pl.pallas_call(
+    vmem = pl.BlockSpec(memory_space=pltpu.VMEM)
+    rows, states = pl.pallas_call(
         functools.partial(fast_kernel, sizes),
         out_shape=(
-            jax.ShapeDtypeStruct((tokens, heads * width), bf16),
-            jax.ShapeDtypeStruct((1, ns, width, width), f32),
+            pltpu.VMEM((tokens, heads * width), bf16),
+            pltpu.VMEM((1, ns, width, width), f32),
         ),
         in_specs=[anywhere] * 5,
-        out_specs=(anywhere, anywhere),
+        out_specs=(vmem, vmem),
         scratch_shapes=[
             pltpu.VMEM((tokens, key_count, width), bf16),
             pltpu.VMEM((tokens, key_count, width), bf16),
@@ -490,6 +502,16 @@
             collective_id=0, has_side_effects=True, vmem_limit_bytes=60 * 1024 * 1024
         ),
     )(query_heads, key_heads, value_heads, gate_log, beta_rate)
+    return pl.pallas_call(
+        hand_over,
+        out_shape=(
+            jax.ShapeDtypeStruct(rows.shape, bf16),
+            jax.ShapeDtypeStruct(states.shape, f32),
+        ),
+        in_specs=[vmem] * 2,
+        out_specs=(anywhere, anywhere),
+        scratch_shapes=[pltpu.SemaphoreType.DMA((2,))],
+    )(rows, states)
 
 
 def choose_device(query_heads, key_heads, value_heads, gate_log, beta_rate):

time: 29.9 us -> 30.6 us (1.023)
  Pallas kernels: 26.8 us -> 28.5 us
  local copies, waits for them, and re-layouts: 2.32 us -> 1.35 us
    pallas_call x1 -> x2, Pallas kernels: 26.8 us -> 28.5 us  [the longest x1 26.7 us: fast_device(): pl.pallas_call(functools.partial(fast_kernel, sizes), out_shape=(pltpu.VM...]
    unnamed x4, local copies, waits for them, and re-layouts: 2.32 us -> 1.35 us
where the time goes in v6:
time: 30.6 us; the launch traced here: 30.5 us
  Pallas kernels  28.5 us (93%)
  local copies, waits for them, and re-layouts  1.35 us (4%)
  between operations  0.65 us (2%)
    pallas_call x1, Pallas kernels, fast_device(): pl.pallas_call(functools.partial(fast_kernel, sizes), out_shape=(pltpu.VM...  26.7 us
    pallas_call x1, Pallas kernels, fast_device(): pl.pallas_call(hand_over, out_shape=(jax.ShapeDtypeStruct(rows.shape, bf1...  1.78 us
    unnamed x4, local copies, waits for them, and re-layouts  1.35 us

profile of v6, /device:TPU:1, one launch (start us, length us, event | category | flops | bytes accessed | tf_op | source)
XLA Modules:
  0.0 30.5 jit_solution(5992585975880202233)
XLA Ops:
  0.6 26.7 %shard_map.68 = (bf16[16,4096]{1,0:T(8,128)(2,1)S(1)}, f32[1,4,128,128]{3,2,1,0:T(8,128)S(1)}) custom-call(bf16[16,16,128]{2,1,0:T(8,128)(2,1)} %q_hbm.1, bf16[16,16,128]{2,1,0:T(8,128)(2,1)} %k_hbm.1, bf16[16,32,128]{2,1,0:T(8,128)(2,1)} %v_hbm.1, bf16[16,32]{1,0:T(8,128)(2,1)} %g_hbm.1, bf16[16,32]{1,0:T(8,128)(2,1)} %b_hbm.1), custom_call_target="tpu_custom_call" | custom-call | tf_op jit(solution)/shard_map/pallas_call | solution.py:467
  27.3 0.0 copy-start
  27.4 0.7 %copy-done = f32[1,4,128,128]{3,2,1,0:T(8,128)} copy-done((f32[1,4,128,128]{3,2,1,0:T(8,128)}, f32[1,4,128,128]{3,2,1,0:T(8,128)S(1)}, u32[]{:S(2)}) %copy-start) | copy-done | bytes 262168
  28.0 0.0 copy-start.1
  28.0 0.7 %copy-done.1 = bf16[16,4096]{1,0:T(8,128)(2,1)} copy-done((bf16[16,4096]{1,0:T(8,128)(2,1)}, bf16[16,4096]{1,0:T(8,128)(2,1)S(1)}, u32[]{:S(2)}) %copy-start.1) | copy-done | bytes 131096
  28.7 1.8 %shard_map.69 = (bf16[16,4096]{1,0:T(8,128)(2,1)}, f32[1,4,128,128]{3,2,1,0:T(8,128)}) custom-call(bf16[16,4096]{1,0:T(8,128)(2,1)} %copy-done.1, f32[1,4,128,128]{3,2,1,0:T(8,128)} %copy-done), custom_call_target="tpu_custom_call" | custom-call | tf_op jit(solution)/shard_map/pallas_call | solution.py:505
Async XLA Ops:
  27.3 0.7 %copy-start = (f32[1,4,128,128]{3,2,1,0:T(8,128)}, f32[1,4,128,128]{3,2,1,0:T(8,128)S(1)}, u32[]{:S(2)}) copy-start(f32[1,4,128,128]{3,2,1,0:T(8,128)S(1)} %get-tuple-element.5.states_in) | copy-start | bytes 786436
  28.0 0.7 %copy-start.1 = (bf16[16,4096]{1,0:T(8,128)(2,1)}, bf16[16,4096]{1,0:T(8,128)(2,1)S(1)}, u32[]{:S(2)}) copy-start(bf16[16,4096]{1,0:T(8,128)(2,1)S(1)} %get-tuple-element.4.rows_in) | copy-start | bytes 393220

commit v7 on v3

--- a/solution.py
+++ b/solution.py
@@ -234,19 +234,22 @@
     for ps, ph in peers[1:]:
         pl.semaphore_signal(barrier, inc=1, device_id=(ps, ph), device_id_type=MESH)
 
-    for load in loads:
-        load.wait()
+    loads[0].wait()
     q_wide[...] = q_in[...].astype(jnp.float32).reshape(tokens * key_heads, width)
+    loads[1].wait()
     k_wide[...] = k_in[...].astype(jnp.float32).reshape(tokens * key_heads, width)
-    v_wide[...] = v_in[...].astype(jnp.float32).reshape(tokens * heads, width)
     for j in range(key_heads):
         queries = q_wide[pl.ds(j, tokens, stride=key_heads), :].astype(jnp.bfloat16)
         keys = k_wide[pl.ds(j, tokens, stride=key_heads), :].astype(jnp.bfloat16)
         send[2 * j, 0:tokens, :] = queries
         send[2 * j + 1, 0:tokens, :] = keys
+    loads[2].wait()
+    v_wide[...] = v_in[...].astype(jnp.float32).reshape(tokens * heads, width)
     for j in range(heads):
         values = v_wide[pl.ds(j, tokens, stride=heads), :].astype(jnp.bfloat16)
         send[j, tokens : 2 * tokens, :] = values
+    loads[3].wait()
+    loads[4].wait()
     both = jnp.concatenate([g_in[...], b_in[...]], axis=0).astype(jnp.float32)
     place_row = lax.broadcasted_iota(jnp.int32, (2 * tokens, width), 0)
     place_col = lax.broadcasted_iota(jnp.int32, (2 * tokens, width), 1)
@@ -257,21 +260,24 @@
 
     pl.semaphore_wait(barrier, ns * nh - 1)
 
-    for i, (ps, ph) in enumerate(peers):
-        j = ph * ns + ps
-        if i == 0:
-            pltpu.make_async_copy(send.at[j], recv.at[s, h], recv_sem.at[0]).start()
-            pltpu.make_async_copy(gb_send.at[j], gb_recv.at[s, h], gb_sem.at[0]).start()
-        else:
-            for source, target, n, sem in ((gb_send, gb_recv, 1, gb_sem), (send, recv, 0, recv_sem)):
-                pltpu.make_async_remote_copy(
-                    src_ref=source.at[j],
-                    dst_ref=target.at[s, h],
-                    send_sem=send_sem.at[n],
-                    recv_sem=sem.at[i // nh],
-                    device_id=(ps, ph),
-                    device_id_type=MESH,
-                ).start()
+    def remote(source, target, n, sem, i):
+        ps, ph = peers[i]
+        pltpu.make_async_remote_copy(
+            src_ref=source.at[ph * ns + ps],
+            dst_ref=target.at[s, h],
+            send_sem=send_sem.at[n],
+            recv_sem=sem.at[i // nh],
+            device_id=(ps, ph),
+            device_id_type=MESH,
+        ).start()
+
+    pltpu.make_async_copy(send.at[mine], recv.at[s, h], recv_sem.at[0]).start()
+    pltpu.make_async_copy(gb_send.at[mine], gb_recv.at[s, h], gb_sem.at[0]).start()
+    for i in range(1, ns * nh):
+        for row in (2 * i - 1, 2 * i):
+            if row < ns * nh:
+                remote(gb_send, gb_recv, 1, gb_sem, row)
+        remote(send, recv, 0, recv_sem, i)
 
     row_ids = lax.broadcasted_iota(jnp.int32, (slab, slab), 0)
     col_ids = lax.broadcasted_iota(jnp.int32, (slab, slab), 1)
@@ -286,20 +292,21 @@
         == lax.broadcasted_iota(jnp.int32, (slab, nh), 1)
     ).astype(jnp.bfloat16)
 
+    for i, at in enumerate(seq_peers):
+        pltpu.make_async_copy(gb_recv.at[at], gb_recv.at[at], gb_sem.at[i]).wait()
+    all_cums, all_betas = [], []
+    for at in seq_peers:
+        rates = dot(expand, gb_recv[at, :, 0, :].astype(jnp.bfloat16))
+        gates = jnp.where(col_ids == token_at, rates, 0.0).astype(jnp.bfloat16)
+        writes = jnp.where(col_ids == token_at + tokens, rates, 0.0).astype(jnp.bfloat16)
+        gate_cols = dot(gates, all_ones).astype(jnp.bfloat16)
+        all_cums.append(dot(lower_ones, gate_cols))
+        all_betas.append(dot(writes, all_ones))
+
     for first in range(0, ns, 2):
         slabs = seq_peers[first : first + 2]
         count = len(slabs)
-        for i, at in enumerate(slabs):
-            pltpu.make_async_copy(gb_recv.at[at], gb_recv.at[at], gb_sem.at[first + i]).wait()
-        cums, betas = [], []
-        for at in slabs:
-            rates = dot(expand, gb_recv[at, :, 0, :].astype(jnp.bfloat16))
-            gates = jnp.where(col_ids == token_at, rates, 0.0).astype(jnp.bfloat16)
-            writes = jnp.where(col_ids == token_at + tokens, rates, 0.0).astype(jnp.bfloat16)
-            gate_cols = dot(gates, all_ones).astype(jnp.bfloat16)
-            cums.append(dot(lower_ones, gate_cols))
-            betas.append(dot(writes, all_ones))
-
+        cums, betas = all_cums[first : first + 2], all_betas[first : first + 2]
         for i, at in enumerate(slabs):
             pltpu.make_async_copy(recv.at[at], recv.at[at], recv_sem.at[first + i]).wait()
             pltpu.make_async_remote_copy(
@@ -355,14 +362,10 @@
                     inverses[n] = inverses[n] + both_products[:slab]
                     powers[n] = both_products[slab:]
             reach *= 2
-        size = small
-        while size < slab:
-            pair = ((row_ids // (2 * size)) == (col_ids // (2 * size))) & (
-                (row_ids // size) != (col_ids // size)
-            )
-            inner = [mul(jnp.where(pair, lowers[n], 0.0), inverses[n]) for n in range(count)]
-            inverses = [inverses[n] - mul(inverses[n], inner[n]) for n in range(count)]
-            size *= 2
+        steps = [mul(inverses[n], jnp.where(same, 0.0, lowers[n])) for n in range(count)]
+        squares = [mul(steps[n], steps[n]) for n in range(count)]
+        inverses = [inverses[n] - mul(steps[n], inverses[n]) for n in range(count)]
+        inverses = [inverses[n] + mul(squares[n], inverses[n]) for n in range(count)]
 
         for n in range(count):
             (queries, keys, values, cum, k_norm, q_norm, cum_row, k_norm_row, beta_row,
@@ -452,14 +455,15 @@
     sizes = (ns, nh, tokens, heads, key_count)
     bf16, f32 = jnp.bfloat16, jnp.float32
     anywhere = pl.BlockSpec(memory_space=pl.ANY)
+    vmem = pl.BlockSpec(memory_space=pltpu.VMEM)
     return pl.pallas_call(
         functools.partial(fast_kernel, sizes),
         out_shape=(
-            jax.ShapeDtypeStruct((tokens, heads * width), bf16),
-            jax.ShapeDtypeStruct((1, ns, width, width), f32),
+            pltpu.VMEM((tokens, heads * width), bf16),
+            pltpu.VMEM((1, ns, width, width), f32),
         ),
         in_specs=[anywhere] * 5,
-        out_specs=(anywhere, anywhere),
+        out_specs=(vmem, vmem),
         scratch_shapes=[
             pltpu.VMEM((tokens, key_count, width), bf16),
             pltpu.VMEM((tokens, key_count, width), bf16),

time: 29.9 us -> 30 us (level)
  Pallas kernels: 26.8 us -> 27.8 us
  local copies, waits for them, and re-layouts: 2.32 us -> 1.36 us
    pallas_call x1, Pallas kernels: 26.8 us -> 27.8 us  [fast_device(): pl.pallas_call(functools.partial(fast_kernel, sizes), out_shape=(pltpu.VM...]
    unnamed x4 -> x2, local copies, waits for them, and re-layouts: 2.32 us -> 1.36 us
where the time goes in v7:
time: 30 us; the launch traced here: 29.8 us
  Pallas kernels  27.8 us (93%)
  local copies, waits for them, and re-layouts  1.36 us (5%)
  between operations  0.64 us (2%)
    pallas_call x1, Pallas kernels, fast_device(): pl.pallas_call(functools.partial(fast_kernel, sizes), out_shape=(pltpu.VM...  27.8 us
    unnamed x2, local copies, waits for them, and re-layouts  1.36 us

profile of v7, /device:TPU:1, one launch (start us, length us, event | category | flops | bytes accessed | tf_op | source)
XLA Modules:
  0.0 29.8 jit_solution(5551701958425204300)
XLA Ops:
  0.6 27.8 %shard_map.68 = (bf16[16,4096]{1,0:T(8,128)(2,1)S(1)}, f32[1,4,128,128]{3,2,1,0:T(8,128)S(1)}) custom-call(bf16[16,16,128]{2,1,0:T(8,128)(2,1)} %q_hbm.1, bf16[16,16,128]{2,1,0:T(8,128)(2,1)} %k_hbm.1, bf16[16,32,128]{2,1,0:T(8,128)(2,1)} %v_hbm.1, bf16[16,32]{1,0:T(8,128)(2,1)} %g_hbm.1, bf16[16,32]{1,0:T(8,128)(2,1)} %b_hbm.1), custom_call_target="tpu_custom_call" | custom-call | tf_op jit(solution)/shard_map/pallas_call | solution.py:459
  28.5 0.7 %copy.9 = bf16[16,4096]{1,0:T(8,128)(2,1)} copy(bf16[16,4096]{1,0:T(8,128)(2,1)S(1)} %get-tuple-element.2) | data formatting | bytes 262144
  29.1 0.7 %copy.10 = f32[1,4,128,128]{3,2,1,0:T(8,128)} copy(f32[1,4,128,128]{3,2,1,0:T(8,128)S(1)} %get-tuple-element.3) | data formatting | bytes 524288

commit v8 on v3

--- a/solution.py
+++ b/solution.py
@@ -234,19 +234,22 @@
     for ps, ph in peers[1:]:
         pl.semaphore_signal(barrier, inc=1, device_id=(ps, ph), device_id_type=MESH)
 
-    for load in loads:
-        load.wait()
+    loads[0].wait()
     q_wide[...] = q_in[...].astype(jnp.float32).reshape(tokens * key_heads, width)
+    loads[1].wait()
     k_wide[...] = k_in[...].astype(jnp.float32).reshape(tokens * key_heads, width)
-    v_wide[...] = v_in[...].astype(jnp.float32).reshape(tokens * heads, width)
     for j in range(key_heads):
         queries = q_wide[pl.ds(j, tokens, stride=key_heads), :].astype(jnp.bfloat16)
         keys = k_wide[pl.ds(j, tokens, stride=key_heads), :].astype(jnp.bfloat16)
         send[2 * j, 0:tokens, :] = queries
         send[2 * j + 1, 0:tokens, :] = keys
+    loads[2].wait()
+    v_wide[...] = v_in[...].astype(jnp.float32).reshape(tokens * heads, width)
     for j in range(heads):
         values = v_wide[pl.ds(j, tokens, stride=heads), :].astype(jnp.bfloat16)
         send[j, tokens : 2 * tokens, :] = values
+    loads[3].wait()
+    loads[4].wait()
     both = jnp.concatenate([g_in[...], b_in[...]], axis=0).astype(jnp.float32)
     place_row = lax.broadcasted_iota(jnp.int32, (2 * tokens, width), 0)
     place_col = lax.broadcasted_iota(jnp.int32, (2 * tokens, width), 1)
@@ -355,14 +358,10 @@
                     inverses[n] = inverses[n] + both_products[:slab]
                     powers[n] = both_products[slab:]
             reach *= 2
-        size = small
-        while size < slab:
-            pair = ((row_ids // (2 * size)) == (col_ids // (2 * size))) & (
-                (row_ids // size) != (col_ids // size)
-            )
-            inner = [mul(jnp.where(pair, lowers[n], 0.0), inverses[n]) for n in range(count)]
-            inverses = [inverses[n] - mul(inverses[n], inner[n]) for n in range(count)]
-            size *= 2
+        steps = [mul(inverses[n], jnp.where(same, 0.0, lowers[n])) for n in range(count)]
+        squares = [mul(steps[n], steps[n]) for n in range(count)]
+        inverses = [inverses[n] - mul(steps[n], inverses[n]) for n in range(count)]
+        inverses = [inverses[n] + mul(squares[n], inverses[n]) for n in range(count)]
 
         for n in range(count):
             (queries, keys, values, cum, k_norm, q_norm, cum_row, k_norm_row, beta_row,
@@ -452,14 +451,15 @@
     sizes = (ns, nh, tokens, heads, key_count)
     bf16, f32 = jnp.bfloat16, jnp.float32
     anywhere = pl.BlockSpec(memory_space=pl.ANY)
+    vmem = pl.BlockSpec(memory_space=pltpu.VMEM)
     return pl.pallas_call(
         functools.partial(fast_kernel, sizes),
         out_shape=(
-            jax.ShapeDtypeStruct((tokens, heads * width), bf16),
-            jax.ShapeDtypeStruct((1, ns, width, width), f32),
+            pltpu.VMEM((tokens, heads * width), bf16),
+            pltpu.VMEM((1, ns, width, width), f32),
         ),
         in_specs=[anywhere] * 5,
-        out_specs=(anywhere, anywhere),
+        out_specs=(vmem, vmem),
         scratch_shapes=[
             pltpu.VMEM((tokens, key_count, width), bf16),
             pltpu.VMEM((tokens, key_count, width), bf16),

time: 29.9 us -> 28.5 us (0.953)
  local copies, waits for them, and re-layouts: 2.32 us -> 1.36 us
  Pallas kernels: 26.8 us -> 26.4 us
    unnamed x4 -> x2, local copies, waits for them, and re-layouts: 2.32 us -> 1.36 us
    pallas_call x1, Pallas kernels: 26.8 us -> 26.4 us  [fast_device(): pl.pallas_call(functools.partial(fast_kernel, sizes), out_shape=(pltpu.VM...]
where the time goes in v8:
time: 28.5 us; the launch traced here: 28.4 us
  Pallas kernels  26.4 us (93%)
  local copies, waits for them, and re-layouts  1.36 us (5%)
  between operations  0.64 us (2%)
    pallas_call x1, Pallas kernels, fast_device(): pl.pallas_call(functools.partial(fast_kernel, sizes), out_shape=(pltpu.VM...  26.4 us
    unnamed x2, local copies, waits for them, and re-layouts  1.36 us

profile of v8, /device:TPU:1, one launch (start us, length us, event | category | flops | bytes accessed | tf_op | source)
XLA Modules:
  0.0 28.4 jit_solution(3730349018816672956)
XLA Ops:
  0.6 26.4 %shard_map.68 = (bf16[16,4096]{1,0:T(8,128)(2,1)S(1)}, f32[1,4,128,128]{3,2,1,0:T(8,128)S(1)}) custom-call(bf16[16,16,128]{2,1,0:T(8,128)(2,1)} %q_hbm.1, bf16[16,16,128]{2,1,0:T(8,128)(2,1)} %k_hbm.1, bf16[16,32,128]{2,1,0:T(8,128)(2,1)} %v_hbm.1, bf16[16,32]{1,0:T(8,128)(2,1)} %g_hbm.1, bf16[16,32]{1,0:T(8,128)(2,1)} %b_hbm.1), custom_call_target="tpu_custom_call" | custom-call | tf_op jit(solution)/shard_map/pallas_call | solution.py:455
  27.0 0.7 %copy.9 = bf16[16,4096]{1,0:T(8,128)(2,1)} copy(bf16[16,4096]{1,0:T(8,128)(2,1)S(1)} %get-tuple-element.2) | data formatting | bytes 262144
  27.7 0.7 %copy.10 = f32[1,4,128,128]{3,2,1,0:T(8,128)} copy(f32[1,4,128,128]{3,2,1,0:T(8,128)S(1)} %get-tuple-element.3) | data formatting | bytes 524288

commit v9 on v8

--- a/solution.py
+++ b/solution.py
@@ -395,6 +395,29 @@
         out_buf[n * nh : (n + 1) * nh] = output.astype(jnp.bfloat16).reshape(nh, tokens, width)
         state_buf[n] = state
 
+        def give(ph):
+            pltpu.make_async_remote_copy(
+                src_ref=out_buf.at[n * nh + ph],
+                dst_ref=out_ref.at[:, columns],
+                send_sem=send_sem.at[2],
+                recv_sem=back_sem.at[0],
+                device_id=(n, ph),
+                device_id_type=MESH,
+            ).start()
+
+        for dh in range(1, nh):
+            give(lax.rem(h + dh, nh))
+
+        @pl.when(s == n)
+        def _():
+            pltpu.make_async_copy(
+                out_buf.at[n * nh + h], out_ref.at[:, columns], back_sem.at[0]
+            ).start()
+
+        @pl.when(s != n)
+        def _():
+            give(h)
+
         @pl.when(s == n)
         def _():
             pltpu.make_async_copy(state_buf.at[n], states_ref.at[0, s], back_sem.at[1]).start()
@@ -409,29 +432,6 @@
                 device_id=(n, h),
                 device_id_type=MESH,
             ).start()
-
-        def give(ph):
-            pltpu.make_async_remote_copy(
-                src_ref=out_buf.at[n * nh + ph],
-                dst_ref=out_ref.at[:, columns],
-                send_sem=send_sem.at[2],
-                recv_sem=back_sem.at[0],
-                device_id=(n, ph),
-                device_id_type=MESH,
-            ).start()
-
-        for dh in range(1, nh):
-            give(lax.rem(h + dh, nh))
-
-        @pl.when(s == n)
-        def _():
-            pltpu.make_async_copy(
-                out_buf.at[n * nh + h], out_ref.at[:, columns], back_sem.at[0]
-            ).start()
-
-        @pl.when(s != n)
-        def _():
-            give(h)
 
     others = pl.ds(0, ns * nh - 1)
     pltpu.make_async_copy(send.at[others], send.at[others], send_sem.at[0]).wait()

time: 28.5 us -> 27.4 us (0.961)
  Pallas kernels: 26.4 us -> 25.1 us
    pallas_call x1, Pallas kernels: 26.4 us -> 25.1 us  [fast_device(): pl.pallas_call(functools.partial(fast_kernel, sizes), out_shape=(pltpu.VM...]
where the time goes in v9:
time: 27.4 us; the launch traced here: 27.1 us
  Pallas kernels  25.1 us (92%)
  local copies, waits for them, and re-layouts  1.36 us (5%)
  between operations  0.64 us (2%)
    pallas_call x1, Pallas kernels, fast_device(): pl.pallas_call(functools.partial(fast_kernel, sizes), out_shape=(pltpu.VM...  25.1 us
    unnamed x2, local copies, waits for them, and re-layouts  1.36 us

profile of v9, /device:TPU:1, one launch (start us, length us, event | category | flops | bytes accessed | tf_op | source)
XLA Modules:
  0.0 27.1 jit_solution(3490758938173007326)
XLA Ops:
  0.6 25.1 %shard_map.68 = (bf16[16,4096]{1,0:T(8,128)(2,1)S(1)}, f32[1,4,128,128]{3,2,1,0:T(8,128)S(1)}) custom-call(bf16[16,16,128]{2,1,0:T(8,128)(2,1)} %q_hbm.1, bf16[16,16,128]{2,1,0:T(8,128)(2,1)} %k_hbm.1, bf16[16,32,128]{2,1,0:T(8,128)(2,1)} %v_hbm.1, bf16[16,32]{1,0:T(8,128)(2,1)} %g_hbm.1, bf16[16,32]{1,0:T(8,128)(2,1)} %b_hbm.1), custom_call_target="tpu_custom_call" | custom-call | tf_op jit(solution)/shard_map/pallas_call | solution.py:455
  25.7 0.7 %copy.9 = bf16[16,4096]{1,0:T(8,128)(2,1)} copy(bf16[16,4096]{1,0:T(8,128)(2,1)S(1)} %get-tuple-element.2) | data formatting | bytes 262144
  26.4 0.7 %copy.10 = f32[1,4,128,128]{3,2,1,0:T(8,128)} copy(f32[1,4,128,128]{3,2,1,0:T(8,128)S(1)} %get-tuple-element.3) | data formatting | bytes 524288
